TPU v7x, 128 devices: a whole 4x4x4 slice. The times are simulated.
128 devices in a mesh: ctx: 8 (over z_hi, x), tp: 8 (over y, core), section: 2 (over z_lo).
Axes of the slice: x: 4, y: 4, z: 4 (z_hi: 2, z_lo: 2; z = z_hi * 2 + z_lo), core: 2. Of those that a mesh axis runs over, the one named last changes fastest.
Arguments:
- prompt_mixer: bfloat16 [8192, 16384], P(('ctx', 'section'), 'tp'), may hold values from -5 to 5
- prompt_gates: bfloat16 [8192, 16384], P(('ctx', 'section'), 'tp'), may hold values from -5 to 5
- prompt_write: bfloat16 [8192, 2048], P(('ctx', 'section'), 'tp'), may hold values from -5 to 5
- prompt_read: bfloat16 [8192, 2048], P(('ctx', 'section'), 'tp'), may hold values from -1 to 1
- prompt_steps: float32 [8192, 256], P(('ctx', 'section'), 'tp'), may hold values from 0 to 1, as said below
- decay_logs: float32 [256], P('tp'), may hold values from -12 to 0
- skip_weights: float32 [256], P('tp'), may hold values from 0.5 to 1.5
- norm_gains: float32 [16384], P('tp'), may hold values from 0.1 to 1.9
- prompt_keys: bfloat16 [8192, 1024], P(('ctx', 'section'), 'tp'), may hold values from -4 to 4
- prompt_values: bfloat16 [8192, 1024], P(('ctx', 'section'), 'tp'), may hold values from -5 to 5
- page_counts: int32 [128], replicated, may hold values from 1 to 16, as said below
- decode_mixer: bfloat16 [128, 4, 16384], P(('ctx', 'section'), None, 'tp'), may hold values from -5 to 5
- decode_gates: bfloat16 [128, 4, 16384], P(('ctx', 'section'), None, 'tp'), may hold values from -5 to 5
- decode_write: bfloat16 [128, 4, 2048], P(('ctx', 'section'), None, 'tp'), may hold values from -5 to 5
- decode_read: bfloat16 [128, 4, 2048], P(('ctx', 'section'), None, 'tp'), may hold values from -1 to 1
- decode_steps: float32 [128, 4, 256], P(('ctx', 'section'), None, 'tp'), may hold values from 0 to 1, as said below
- decode_queries: bfloat16 [128, 4, 8192], P(('ctx', 'section'), None, 'tp'), may hold values from -150 to 150
- decode_keys: bfloat16 [128, 4, 1024], P(('ctx', 'section'), None, 'tp'), may hold values from -5 to 5
- decode_values: bfloat16 [128, 4, 1024], P(('ctx', 'section'), None, 'tp'), may hold values from -5 to 5
- mixer_output: bfloat16 [16384, 8192], P('tp', ('ctx', 'section')), may hold values from -0.046875 to 0.046875
- attend_output: bfloat16 [8192, 8192], P('tp', ('ctx', 'section')), may hold values from -0.0625 to 0.0625
Outputs:
- prompt_mixed: bfloat16 [8192, 16384], P(('ctx', 'section'), 'tp')
- decode_mixed: bfloat16 [128, 4, 8192], P('tp', None, ('ctx', 'section'))
Inputs may be any that keep to these rules, and one draw needn't show every extreme that they name: `page_counts`: every row continues at least one page; some row continues all 16 pages and some row exactly one. `prompt_steps`: positive. `decode_steps`: positive.
All inputs are finite; a program needn't handle non-finite values.
Results may differ from a plain program's by a relative error of at most 0.02.
Values may be sent and summed in bfloat16 or wider, within the bound.
A program may use at most 320 MiB of HBM per device.

v0:
```python
from functools import partial

import jax
import jax.numpy as jnp
from jax import lax
from jax.sharding import PartitionSpec as P

HEADS = 256
HEAD_DIM = 64
STATE = 256
GROUPS = 8
QHEADS = 64
KV_HEADS = 8
ATT_DIM = 128
STEPS = 4
BLOCK = 256


HIGH = lax.Precision.HIGHEST
EPS = 1e-05
NEG = -1e30


def prefix(value, axis, combine, identity):
    peers, index = (lax.axis_size(axis), lax.axis_index(axis))
    everything = jax.tree.map(
        lambda part, kind: lax.all_gather(part.astype(kind), axis),
        value,
        (jnp.bfloat16, jnp.bfloat16),
    )
    start = jax.tree.map(
        lambda part, zero: jnp.broadcast_to(jnp.asarray(zero, part.dtype), part.shape),
        value,
        identity,
    )

    def step(k, before):
        reached = k < index
        new = combine(
            before, jax.tree.map(lambda part, own: part[k].astype(own.dtype), everything, value)
        )
        return jax.tree.map(lambda a, b: jnp.where(reached, a, b), new, before)

    return lax.fori_loop(0, peers, step, start)


def ssd_block(decay_rate, per_group, carried, inputs):
    x_block, b_block, c_block, dt_block = inputs
    log_decay = jnp.cumsum(-dt_block * decay_rate, axis=0)
    block_len = x_block.shape[0]
    lower_mask = jnp.arange(block_len)[:, None] >= jnp.arange(block_len)[None, :]
    decay_gap = log_decay.T[:, :, None] - log_decay.T[:, None, :]
    lower_decay = jnp.where(lower_mask[None], jnp.exp(jnp.minimum(decay_gap, 0.0)), 0.0)
    affinity = jnp.einsum("qgn,kgn->gqk", c_block, b_block, precision=HIGH)
    affinity = jnp.repeat(affinity, per_group, axis=0)
    mixing = lower_decay * affinity * dt_block.T[:, None, :]
    out_block = jnp.einsum("hqk,khp->qhp", mixing, x_block, precision=HIGH)
    read_heads = jnp.repeat(c_block, per_group, axis=1)
    write_heads = jnp.repeat(b_block, per_group, axis=1)
    out_block = out_block + jnp.exp(log_decay)[:, :, None] * jnp.einsum(
        "qhn,hpn->qhp", read_heads, carried, precision=HIGH
    )
    tail_weight = jnp.exp(log_decay[-1][None, :] - log_decay) * dt_block
    fresh_state = jnp.einsum(
        "khp,khn->hpn", x_block * tail_weight[:, :, None], write_heads, precision=HIGH
    )
    carried = jnp.exp(log_decay[-1])[:, None, None] * carried + fresh_state
    return (carried, out_block)


def gated_norm(values, gates, gains, group_count):
    leading = values.shape[:-2]
    gated = values.reshape(leading + (-1,)) * jax.nn.silu(gates.astype(jnp.float32))
    grouped = gated.reshape(leading + (group_count, -1))
    scaled = grouped * lax.rsqrt(jnp.mean(grouped * grouped, axis=-1, keepdims=True) + EPS)
    return (scaled.reshape(leading + (-1,)) * gains).astype(jnp.bfloat16)


def compose(earlier, later):
    return (earlier[0] * later[0], later[0][:, None, None] * earlier[1] + later[1])


def merge_parts(first, second):
    top = jnp.maximum(first[0], second[0])
    first_scale = jnp.exp(first[0] - top)
    second_scale = jnp.exp(second[0] - top)
    return (
        top,
        first[1] * first_scale + second[1] * second_scale,
        first[2] * first_scale[..., None] + second[2] * second_scale[..., None],
    )


def partial_attend(queries, keys, values, visible):
    scale = queries.shape[-1] ** (-0.5)
    scores = (
        jnp.einsum("rskga,tka->rskgt", queries, keys, preferred_element_type=jnp.float32) * scale
    )
    scores = jnp.where(visible, scores, NEG)
    top = jnp.max(scores, axis=-1)
    weights = jnp.where(visible, jnp.exp(scores - top[..., None]), 0.0)
    total = jnp.sum(weights, axis=-1)
    summed = jnp.einsum(
        "rskgt,tka->rskga", weights.astype(jnp.bfloat16), values, preferred_element_type=jnp.float32
    )
    return (top, total, summed)


def on_device(
    prompt_mixer,
    prompt_gates,
    prompt_write,
    prompt_read,
    prompt_steps,
    decay_logs,
    skip_weights,
    norm_gains,
    prompt_keys,
    prompt_values,
    page_counts,
    decode_mixer,
    decode_gates,
    decode_write,
    decode_read,
    decode_steps,
    decode_queries,
    decode_keys,
    decode_values,
    mixer_output,
    attend_output,
):
    per_group = HEADS // GROUPS
    heads_here = decay_logs.shape[0]
    groups_here = heads_here // per_group
    tokens_here = prompt_mixer.shape[0]
    block_count = tokens_here // BLOCK
    decay_rate = jnp.exp(decay_logs)
    position = lax.axis_index(("ctx", "section"))
    shard_total = lax.axis_size(("ctx", "section"))
    mixer_flat = prompt_mixer.astype(jnp.float32).reshape(tokens_here, heads_here, HEAD_DIM)
    write_flat = prompt_write.astype(jnp.float32).reshape(tokens_here, groups_here, STATE)
    read_flat = prompt_read.astype(jnp.float32).reshape(tokens_here, groups_here, STATE)
    inputs = (
        mixer_flat.reshape(block_count, BLOCK, heads_here, HEAD_DIM),
        write_flat.reshape(block_count, BLOCK, groups_here, STATE),
        read_flat.reshape(block_count, BLOCK, groups_here, STATE),
        prompt_steps.reshape(block_count, BLOCK, heads_here),
    )
    zero_state = jnp.zeros((heads_here, HEAD_DIM, STATE), jnp.float32)
    local_state, outputs = lax.scan(partial(ssd_block, decay_rate, per_group), zero_state, inputs)
    outputs = outputs.reshape(tokens_here, heads_here, HEAD_DIM)
    shard_log = jnp.cumsum(-prompt_steps * decay_rate, axis=0)
    shard_decay = jnp.exp(shard_log[-1])
    identity = (jnp.ones_like(shard_decay), zero_state)
    before = prefix((shard_decay, local_state), ("ctx", "section"), compose, identity)
    entry_state = before[1]
    after = compose(before, (shard_decay, local_state))[1]
    rounded_states = lax.all_gather(
        after.astype(jnp.bfloat16)[None], ("ctx", "section"), axis=0, tiled=True
    )
    all_states = rounded_states.astype(jnp.float32)
    read_heads = jnp.repeat(read_flat, per_group, axis=1)
    outputs = outputs + jnp.exp(shard_log)[:, :, None] * jnp.einsum(
        "thn,hpn->thp", read_heads, entry_state, precision=HIGH
    )
    outputs = outputs + skip_weights[None, :, None] * mixer_flat
    prompt_mixed = gated_norm(outputs, prompt_gates, norm_gains, groups_here)
    rows_here = decode_mixer.shape[0]
    counts_here = lax.dynamic_slice_in_dim(page_counts, position * rows_here, rows_here)
    choose = (counts_here[:, None] - 1 == jnp.arange(shard_total)[None, :]).astype(jnp.float32)
    carried = jnp.einsum("rk,khpn->rhpn", choose, all_states, precision=HIGH)
    write_dec = jnp.repeat(
        decode_write.astype(jnp.float32).reshape(rows_here, STEPS, groups_here, STATE),
        per_group,
        axis=2,
    )
    read_dec = jnp.repeat(
        decode_read.astype(jnp.float32).reshape(rows_here, STEPS, groups_here, STATE),
        per_group,
        axis=2,
    )
    results = []
    for step_index in range(STEPS):
        mixer_now = (
            decode_mixer[:, step_index].astype(jnp.float32).reshape(rows_here, heads_here, HEAD_DIM)
        )
        dt_now = decode_steps[:, step_index]
        carried = (
            jnp.exp(-dt_now * decay_rate)[:, :, None, None] * carried
            + (dt_now[:, :, None] * mixer_now)[:, :, :, None]
            * write_dec[:, step_index][:, :, None, :]
        )
        results.append(
            jnp.einsum("rhn,rhpn->rhp", read_dec[:, step_index], carried, precision=HIGH)
            + skip_weights[None, :, None] * mixer_now
        )
    ssd_rows = gated_norm(jnp.stack(results, axis=1), decode_gates, norm_gains, groups_here)
    kv_here = decode_keys.shape[-1] // ATT_DIM
    group_size = QHEADS // KV_HEADS
    queries = decode_queries.reshape(rows_here, STEPS, kv_here, group_size, ATT_DIM)
    own_keys = decode_keys.reshape(rows_here, STEPS, kv_here, ATT_DIM)
    own_values = decode_values.reshape(rows_here, STEPS, kv_here, ATT_DIM)
    scale = ATT_DIM ** (-0.5)
    near_scores = (
        jnp.einsum("rskga,rtka->rskgt", queries, own_keys, preferred_element_type=jnp.float32)
        * scale
    )
    causal = (jnp.arange(STEPS)[:, None] >= jnp.arange(STEPS)[None, :])[None, :, None, None, :]
    near_scores = jnp.where(causal, near_scores, NEG)
    near_top = jnp.max(near_scores, axis=-1)
    near_weights = jnp.where(causal, jnp.exp(near_scores - near_top[..., None]), 0.0)
    near_part = (
        near_top,
        jnp.sum(near_weights, axis=-1),
        jnp.einsum(
            "rskgt,rtka->rskga",
            near_weights.astype(jnp.bfloat16),
            own_values,
            preferred_element_type=jnp.float32,
        ),
    )
    limit = counts_here * tokens_here
    stat_shape = (rows_here, STEPS, kv_here, group_size)
    start_part = (
        jnp.full(stat_shape, NEG, jnp.float32),
        jnp.zeros(stat_shape, jnp.float32),
        jnp.zeros(stat_shape + (ATT_DIM,), jnp.float32),
    )
    keys_piece = lax.all_gather(prompt_keys, ("ctx", "section"), axis=0, tiled=True).reshape(
        -1, kv_here, ATT_DIM
    )
    values_piece = lax.all_gather(prompt_values, ("ctx", "section"), axis=0, tiled=True).reshape(
        -1, kv_here, ATT_DIM
    )
    spots = jnp.arange(keys_piece.shape[0])
    visible = (spots[None, :] < limit[:, None])[:, None, None, None, :]
    far_part = merge_parts(start_part, partial_attend(queries, keys_piece, values_piece, visible))
    merged = merge_parts(far_part, near_part)
    att_rows = (merged[2] / merged[1][..., None]).reshape(rows_here, STEPS, -1).astype(jnp.bfloat16)
    features = jnp.concatenate([ssd_rows, att_rows], axis=-1)
    every_row = lax.all_gather(features, ("ctx", "section"), axis=0, tiled=True)
    flat_rows = every_row.reshape(-1, every_row.shape[-1])
    weight = jnp.concatenate([mixer_output, attend_output], axis=0)
    summed = lax.psum_scatter(
        jnp.dot(flat_rows, weight, preferred_element_type=jnp.float32).astype(jnp.bfloat16),
        "tp",
        scatter_dimension=0,
        tiled=True,
    )
    decode_mixed = summed.reshape(-1, STEPS, weight.shape[1])
    return (prompt_mixed, decode_mixed)


def solution(mesh):
    return jax.shard_map(
        on_device,
        mesh=mesh,
        in_specs=(
            P(("ctx", "section"), "tp"),
            P(("ctx", "section"), "tp"),
            P(("ctx", "section"), "tp"),
            P(("ctx", "section"), "tp"),
            P(("ctx", "section"), "tp"),
            P("tp"),
            P("tp"),
            P("tp"),
            P(("ctx", "section"), "tp"),
            P(("ctx", "section"), "tp"),
            P(),
            P(("ctx", "section"), None, "tp"),
            P(("ctx", "section"), None, "tp"),
            P(("ctx", "section"), None, "tp"),
            P(("ctx", "section"), None, "tp"),
            P(("ctx", "section"), None, "tp"),
            P(("ctx", "section"), None, "tp"),
            P(("ctx", "section"), None, "tp"),
            P(("ctx", "section"), None, "tp"),
            P("tp", ("ctx", "section")),
            P("tp", ("ctx", "section")),
        ),
        out_specs=(P(("ctx", "section"), "tp"), P("tp", None, ("ctx", "section"))),
        check_vma=False,
    )
```

profile of v0, /device:TPU:0, one launch (start us, length us, event | category | flops | bytes accessed | tf_op | source)
XLA Modules:
  0.0 1298.1 jit_solution(3692967389823227537)
XLA Ops:
  8.8 7.4 reshape.540
  16.2 7.9 copy.106
  24.9 152.5 %while.27 = (s32[]{:T(128)}, f32[32,64,256]{2,1,0:T(8,128)S(1)}, f32[2,256,32,64]{1,0,3,2:T(2,128)}, f32[2,256,32]{1,0,2:T(2,128)S(1)}, f32[32]{0:T(128)S(1)}, /...) while((s32[]{:T(128)}, f32[32,64,256]{2,1,0:T(8,128)S(1)}, ...), condition=%wide.region_3.4_spmd.clone, body=%wide.region_0.3_spmd.clone.sunk | while | flops 5048475648 | bytes 45878892 | solution.py:150
  28.3 12.1 fusion.180
  40.6 9.4 fusion.181
  58.3 42.8 %dynamic_update_slice.6 = f32[2,256,32,64]{1,0,3,2:T(2,128)} dynamic-update-slice(f32[2,256,32,64]{1,0,3,2:T(2,128)} %get-tuple-element.389, f32[1,256,32,64]{1,0,3,2:T(1,128)} %copy.218, s32[]{:T(128)S(6)} %copy.223, s32[]{:T(128)} %constant.54.clone.1..sunk, s32[]{:T(128)} %constant.54.clone.1..sunk, s32[]{:T(128)} %constant.54.clone.1..sunk) | dynamic-update-slice | bytes 4194308 | tf_op jit(solution)/shard_map/while/body/jit(dynamic_update_index_in_dim)/dynamic_update_slice | solution.py:150
  104.1 12.1 fusion.180
  116.5 9.4 fusion.181
  134.1 42.8 %dynamic_update_slice.6 = f32[2,256,32,64]{1,0,3,2:T(2,128)} dynamic-update-slice(f32[2,256,32,64]{1,0,3,2:T(2,128)} %get-tuple-element.389, f32[1,256,32,64]{1,0,3,2:T(1,128)} %copy.218, s32[]{:T(128)S(6)} %copy.223, s32[]{:T(128)} %constant.54.clone.1..sunk, s32[]{:T(128)} %constant.54.clone.1..sunk, s32[]{:T(128)} %constant.54.clone.1..sunk) | dynamic-update-slice | bytes 4194308 | tf_op jit(solution)/shard_map/while/body/jit(dynamic_update_index_in_dim)/dynamic_update_slice | solution.py:150
  182.1 48.7 %all-gather.2 = bf16[16,1,32]{2,1,0:T(2,128)(2,1)S(1)} all-gather(bf16[1,1,32]{2,1,0:T(2,128)(2,1)S(1)} %bitcast.310), channel_id=1, replica_groups=mesh['ctx'=8,'tp'=8,'section'=2] {'ctx','section'}, dimensions={0}, use_global_device_ids=true | all-gather | bytes 1088 | tf_op jit(solution)/shard_map/all_gather | solution.py:27
  230.8 296.1 %all-gather.15.cloned.1.call-done = bf16[512,64,256]{2,1,0:T(8,128)(2,1)} async-done(((bf16[32,64,256]{2,1,0:T(8,128)(2,1)}), bf16[512,64,256]{2,1,0:T(8,128)(2,1)}) %all-gather.15.cloned.1.call-update) | async-done | bytes 16777232 | tf_op jit(solution)/shard_map/all_gather | solution.py:27
  526.9 56.6 %while.28 = (s32[]{:T(128)}, f32[32,64,256]{2,1,0:T(8,128)}, s32[]{:T(128)}, bf16[16,32]{1,0:T(8,128)(2,1)S(1)}, bf16[16,32,64,256]{3,2,1,0:T(8,128)(2,1)}, /*index=5*/s32[]{:T(128)}, s32[]{:T(128)}) while((s32[]{:T(128)}, f32[32,64,256]{2,1,0:T(8,128)}, s32[]{:T(128)}, bf16[16,32]{1,0:T(8,128)(2,1)S(1)}, ...), condition=%wide.region_7.8_spmd.clone, body=%wide.region_6.7_spmd.clone.sunk | while | flops 2621476 | bytes 5243313 | solution.py:44
  596.3 17.3 %all-gather.9.cloned.1.call-done = bf16[8192,128]{1,0:T(8,128)(2,1)} async-done(((bf16[512,128]{1,0:T(8,128)(2,1)}), bf16[8192,128]{1,0:T(8,128)(2,1)}) %all-gather.9.cloned.1.call-update) | async-done | bytes 2097168 | tf_op jit(solution)/shard_map/all_gather | solution.py:229
  620.1 71.5 %all-gather.11.cloned.1.call-done = bf16[8192,128]{1,0:T(8,128)(2,1)} async-done(((bf16[512,128]{1,0:T(8,128)(2,1)}), bf16[8192,128]{1,0:T(8,128)(2,1)}) %all-gather.11.cloned.1.call-update) | async-done | bytes 2097168 | tf_op jit(solution)/shard_map/all_gather | solution.py:232
  697.2 341.3 %all-gather.17.cloned.1.call-done = bf16[512,64,256]{2,1,0:T(8,128)(2,1)} async-done(((bf16[32,64,256]{2,1,0:T(8,128)(2,1)}), bf16[512,64,256]{2,1,0:T(8,128)(2,1)}) %all-gather.17.cloned.1.call-update) | async-done | bytes 16777232 | tf_op jit(solution)/shard_map/all_gather | solution.py:158
  1038.5 28.0 %multiply_add_fusion.1 = (f32[8,32,64,256]{3,0,2,1:T(8,128)S(1)}, f32[8,32,64,256]{3,0,2,1:T(8,128)}, f32[8,32,64,256]{3,0,2,1:T(8,128)}, f32[8,32,64,256]{3,0,2,1:T(8,128)}) fusion(f32[8,256]{1,0:T(8,128)} %get-tuple-element.260, f32[8,32,64]{0,2,1:T(8,128)S(1)} %copy.125, f32[8,32]{0,1:T(8,128)} %copy.124, f32[8,256]{1,0:T(8,128)} %get-tuple-element.261, ...), kind=kOutput, calls=%fused_computation.62 | convolution fusion | flops 184549504 | bytes 84185120 | tf_op jit(solution)/shard_map/rk,khpn->rhpn/dot_general | solution.py:171
  1066.5 22.7 %fusion.46 = f32[8,32,1,64]{3,2,1,0:T(1,128)S(1)} fusion(f32[8,32,64,256]{3,0,2,1:T(8,128)} %get-tuple-element.283, f32[8,256]{1,0:T(8,128)S(1)} %get-tuple-element.255), kind=kOutput, calls=%fused_computation.58 | convolution fusion | flops 50331648 | bytes 16850944 | tf_op jit(solution)/shard_map/rhn,rhpn->rhp/dot_general | solution.py:194
  1089.3 22.7 %fusion.44 = f32[8,32,1,64]{3,2,1,0:T(1,128)S(1)} fusion(f32[8,32,64,256]{3,0,2,1:T(8,128)} %get-tuple-element.245, f32[8,256]{1,0:T(8,128)S(1)} %get-tuple-element.258), kind=kOutput, calls=%fused_computation.56 | convolution fusion | flops 50331648 | bytes 16850944 | tf_op jit(solution)/shard_map/rhn,rhpn->rhp/dot_general | solution.py:194
  1112.0 22.9 %fusion.42 = f32[8,32,1,64]{3,2,1,0:T(1,128)S(1)} fusion(f32[8,32,64,256]{3,0,2,1:T(8,128)} %get-tuple-element.244, f32[8,256]{1,0:T(8,128)S(1)} %get-tuple-element.257), kind=kOutput, calls=%fused_computation.54 | convolution fusion | flops 50331648 | bytes 16850944 | tf_op jit(solution)/shard_map/rhn,rhpn->rhp/dot_general | solution.py:194
  1135.0 17.2 %fusion.40 = f32[8,32,1,64]{3,2,1,0:T(1,128)S(1)} fusion(f32[8,32,64,256]{3,0,2,1:T(8,128)S(1)} %get-tuple-element.243, f32[8,256]{1,0:T(8,128)S(1)} %get-tuple-element.256), kind=kOutput, calls=%fused_computation.52 | convolution fusion | flops 50331648 | bytes 16850944 | tf_op jit(solution)/shard_map/rhn,rhpn->rhp/dot_general | solution.py:194
  1160.3 6.6 reshape.485
  1167.0 18.9 %fusion.66 = f32[512,32,64]{0,2,1:T(8,128)} fusion(f32[512,32,64]{0,2,1:T(8,128)} %reshape.485, f32[512,32,64]{0,2,1:T(8,128)} %bitcast.289, f32[32,64,256]{2,1,0:T(8,128)S(1)} %copy-done.2, f32[512,256]{1,0:T(8,128)S(1)} %bitcast.293, f32[32]{0:T(128)S(1)} %copy-done.22, f32[512,32]{0,1:T(8,128)S(1)} %fusion.144), kind=kOutput, calls=%fused_computation.84 | convolution fusion | flops 3225419776 | bytes 15270016 | tf_op jit(solution)/shard_map/thn,hpn->thp/dot_general | solution.py:163
  1191.3 55.1 %all-gather.13.cloned.1.call-done = bf16[128,4,3072]{2,0,1:T(8,128)(2,1)} async-done(((bf16[8,4,3072]{2,0,1:T(8,128)(2,1)}), bf16[128,4,3072]{2,0,1:T(8,128)(2,1)}) %all-gather.13.cloned.1.call-update) | async-done | bytes 3145744 | tf_op jit(solution)/shard_map/all_gather | solution.py:241
  1265.9 23.7 %reduce-scatter.2.cloned.1.call-done = bf16[64,512]{1,0:T(8,128)(2,1)} async-done(((bf16[512,512]{1,0:T(8,128)(2,1)}), bf16[64,512]{1,0:T(8,128)(2,1)}) %reduce-scatter.2.cloned.1.call-update) | async-done | bytes 65552 | tf_op jit(solution)/shard_map/reduce_scatter | solution.py:244
  (209 shorter events, 145.9 us)
Async XLA Ops:
  7.2 689.7 %copy-start = (bf16[8,4,128]{2,1,0:T(4,128)(2,1)S(1)}, bf16[8,4,128]{2,1,0:T(4,128)(2,1)}, u32[]{:S(2)}) copy-start(bf16[8,4,128]{2,1,0:T(4,128)(2,1)} %param.43) | copy-start | bytes 24580
  7.2 519.8 %all-gather.15.cloned.1.call-start = ((), (), s32[]{:S(2)}) async-start(), calls=%async_computation.5 | async-start | bytes 17825792 | tf_op jit(solution)/shard_map/all_gather | solution.py:27
  16.2 7.9 copy-start.11
  16.2 8.7 copy-start.12
  40.6 9.4 copy-start.3
  54.8 46.3 %copy-start.9 = (f32[2,256,32]{1,0,2:T(2,128)S(1)}, f32[2,256,32]{1,0,2:T(2,128)}, u32[]{:S(2)}) copy-start(f32[2,256,32]{1,0,2:T(2,128)} %copy-done.8) | copy-start | bytes 196612 | tf_op jit(solution)/shard_map/while
  116.5 9.4 copy-start.3
  130.7 46.3 %copy-start.9 = (f32[2,256,32]{1,0,2:T(2,128)S(1)}, f32[2,256,32]{1,0,2:T(2,128)}, u32[]{:S(2)}) copy-start(f32[2,256,32]{1,0,2:T(2,128)} %copy-done.8) | copy-start | bytes 196612 | tf_op jit(solution)/shard_map/while
  178.6 435.0 %all-gather.9.cloned.1.call-start = ((), (), s32[]{:S(2)}) async-start(), calls=%async_computation.1 | async-start | bytes 2228224 | tf_op jit(solution)/shard_map/all_gather | solution.py:229
  179.4 512.2 %all-gather.11.cloned.1.call-start = ((), (), s32[]{:S(2)}) async-start(), calls=%async_computation.2 | async-start | bytes 2228224 | tf_op jit(solution)/shard_map/all_gather | solution.py:232
  180.1 858.4 %all-gather.17.cloned.1.call-start = ((), (), s32[]{:S(2)}) async-start(), calls=%async_computation.6 | async-start | bytes 17825792 | tf_op jit(solution)/shard_map/all_gather | solution.py:158
  181.6 345.3 %copy-start.16 = (f32[32,4]{0,1:T(4,128)}, f32[32,4]{0,1:T(4,128)S(1)}, u32[]{:S(2)}) copy-start(f32[32,4]{0,1:T(4,128)S(1)} %slice.76) | copy-start | bytes 1540
  586.5 7.9 copy-start.25
  586.5 8.5 copy-start.26
  586.5 9.1 copy-start.18
  586.5 9.7 copy-start.19
  586.5 659.9 %all-gather.13.cloned.1.call-start = ((), (), s32[]{:S(2)}) async-start(), calls=%async_computation.3 | async-start | bytes 3342336 | tf_op jit(solution)/shard_map/all_gather | solution.py:241
  1135.0 17.2 %copy-start.21 = (f32[32]{0:T(128)S(1)}, f32[32]{0:T(128)}, u32[]{:S(2)}) copy-start(f32[32]{0:T(128)} %param.31) | copy-start | bytes 388
  1135.0 21.5 %copy-start.15 = (f32[2048]{0:T(1024)S(1)}, f32[2048]{0:T(1024)}, u32[]{:S(2)}) copy-start(f32[2048]{0:T(1024)} %param.32) | copy-start | bytes 24580
  1157.3 132.3 %reduce-scatter.2.cloned.1.call-start = ((), (), s32[]{:S(2)}) async-start(), calls=%async_computation.4 | async-start | bytes 589824 | tf_op jit(solution)/shard_map/reduce_scatter | solution.py:244
  1160.3 6.6 copy-start.17
  1160.3 6.7 copy-start.2
  1160.3 6.7 copy-start.22
  1262.8 28.3 %copy-start.1 = (bf16[8,4,128]{2,1,0:T(4,128)(2,1)S(1)}, bf16[8,4,128]{2,1,0:T(4,128)(2,1)}, u32[]{:S(2)}) copy-start(bf16[8,4,128]{2,1,0:T(4,128)(2,1)} %param.43) | copy-start | bytes 24580
  (12 other events, 39.0 us)
Sparse Core Ops, SparseCore 0:
  178.7 348.1 all-gather.14
  528.6 85.0 all-gather.8
  615.3 76.2 all-gather.10
  693.1 345.4 all-gather.16
  1157.4 89.0 all-gather.12
  1259.1 30.4 reduce-scatter.1
where the time goes:
time: 1310 us; the launch traced here: 1300 us
  waiting for transfers between devices  806 us (62%)
  matrix products  201 us (15%)
  local copies, waits for them, and re-layouts  148 us (11%)
  other arithmetic  78.8 us (6%)
  blocking collectives  48.7 us (4%)
  between operations  14.7 us (1%)
    all_gather x1, waiting for transfers between devices, on_device(): lax.all_gather(after.astype(jnp.bfloat16)[None], ('ctx', 'section'), axis...  341 us
    all_gather x1, waiting for transfers between devices, prefix(): lax.all_gather(part.astype(kind), axis)  296 us
    dynamic_update_slice x4, local copies, waits for them, and re-layouts, on_device(): lax.scan(partial(ssd_block, decay_rate, per_group), zero_state, inputs)  92.5 us
    dot_general x4, matrix products, on_device(): jnp.einsum('rhn,rhpn->rhp', read_dec[:, step_index], carried, precision=H...  85.6 us
    all_gather x1, waiting for transfers between devices, on_device(): lax.all_gather(prompt_values, ('ctx', 'section'), axis=0, tiled=True)  71.5 us
    select_n x16, other arithmetic, step(): return jax.tree.map(lambda a, b: jnp.where(reached, a, b), new, before)  56.5 us
    all_gather x1, waiting for transfers between devices, on_device(): every_row = lax.all_gather(features, ('ctx', 'section'), axis=0, tiled=True)  55.1 us
    all_gather x1, blocking collectives, prefix(): lax.all_gather(part.astype(kind), axis)  48.7 us
  transfers between devices with their start and end apart: 6, of which 6 were waited for; matrix products, arithmetic and copies ran while one was open for 9% of the time, Pallas kernels for 0%

commit v1 on v0

v1 whole, which is shorter than its diff:
```python
import jax
import jax.numpy as jnp
from jax import lax
from jax.experimental import pallas as pl
from jax.experimental.pallas import tpu as pltpu
from jax.sharding import PartitionSpec as P

HEADS, HEAD_DIM, STATE, GROUPS = 256, 64, 256, 8
QHEADS, KV_HEADS, ATT_DIM, STEPS = 64, 8, 128, 4
EPS = 1e-05
NEG = -1e30
F32, BF16 = jnp.float32, jnp.bfloat16
MESH = pl.DeviceIdType.MESH

PAGES = 16
TOK = 512
HL = 32
FEAT = HL * HEAD_DIM
ROWS = 8
RS = ROWS * STEPS
CH = 128
NCH = TOK // CH
QH = QHEADS // KV_HEADS
NQ = QH * RS
TILE = 256
NT = FEAT // TILE
COLS = 512
TP = 8
ALLF = FEAT + QH * ATT_DIM
SCALE = ATT_DIM ** -0.5


def dot(a, b):
    return jnp.dot(a, b, preferred_element_type=F32)


def dot_t(a, b):
    return lax.dot_general(a, b, (((1,), (1,)), ((), ())), preferred_element_type=F32)


def dot_tn(a, b):
    return lax.dot_general(a, b, (((0,), (0,)), ((), ())), preferred_element_type=F32)


def split2(v):
    hi = v.astype(BF16)
    return hi, (v - hi.astype(F32)).astype(BF16)


def split3(v):
    hi = v.astype(BF16)
    rest = v - hi.astype(F32)
    mid = rest.astype(BF16)
    return hi, mid, (rest - mid.astype(F32)).astype(BF16)


def place(p):
    return {"ctx": p // 2, "section": lax.rem(p, 2)}


def spot(x, z):
    return (z // 2) * 8 + x * 2 + lax.rem(z, 2)


def remote(src, dst, send, recv, device):
    return pltpu.make_async_remote_copy(
        src_ref=src, dst_ref=dst, send_sem=send, recv_sem=recv, device_id=device, device_id_type=MESH
    )


def kernel(
    x, gate, bm, cm, dt, dlog, skip, gains, keys, values, counts,
    xd, gd, bd, cd, dtd, qd, kd, vd, w1, w2,
    out, dec,
    kbuf, vbuf, qbuf, cbuf, s_send, s_recv, pst, e_recv, sc_send, sc_recv,
    o_send, o_recv, t_send, t_recv, feat, p_send, p_recv,
    exp_m, bt, mixg, a_hi, a_lo, b_hi, b_lo, small, rows, xp, chunk_s, yi, av, sq, fac,
    scores, acc, cntb, flat_x, flat_g, flat_b, flat_c, flat_dt, flat_q, flat_k, flat_v, ud,
    kv_ss, kv_rs, q_ss, q_rs, c_ss, c_rs, s_ss, s_rs, e_ss, e_rs, sc_ss, sc_rs,
    o_ss, o_rs, t_ss, t_rs, f1_ss, f1_rs, f2_ss, f2_rs, h1_ss, h1_rs, h2_ss, h2_rs, p_ss, p_rs,
):
    me = lax.axis_index("ctx") * 2 + lax.axis_index("section")
    tp = lax.axis_index("tp")
    xi = lax.rem(me // 2, 4)
    zi = (me // 8) * 2 + lax.rem(me, 2)

    def xpeer(d):
        return lax.rem(xi + d, 4)

    def zpeer(d):
        return lax.rem(zi + d, 4)

    barrier = pltpu.get_barrier_semaphore()

    def greet(d, c):
        pl.semaphore_signal(barrier, inc=1, device_id=place(lax.rem(me + d, PAGES)), device_id_type=MESH)
        return c

    def greet_tp(d, c):
        pl.semaphore_signal(barrier, inc=1, device_id={"tp": lax.rem(tp + d, TP)}, device_id_type=MESH)
        return c

    lax.fori_loop(1, PAGES, greet, 0)
    lax.fori_loop(1, TP, greet_tp, 0)

    for r in range(ROWS):
        sl = slice(r * STEPS, (r + 1) * STEPS)
        flat_q[sl, :] = qd[r].astype(F32)
        flat_c[sl, :] = cd[r].astype(F32)
    for h in range(QH):
        qbuf[xi, h * RS:(h + 1) * RS, :] = flat_q[:, h * ATT_DIM:(h + 1) * ATT_DIM].astype(BF16)
    cbuf[me] = flat_c[...].astype(BF16)

    pl.semaphore_wait(barrier, PAGES - 1 + TP - 1)

    kv_send, q_send = [], []
    for d in (1, 3, 2):
        dz = place(spot(xi, zpeer(d)))
        dx = place(spot(xpeer(d), zi))
        for i, (src, dst) in enumerate(((keys, kbuf), (values, vbuf))):
            cp = remote(src, dst.at[zi], kv_ss.at[i, d], kv_rs.at[i, d], dz)
            cp.start()
            kv_send.append(cp)
        cp = remote(qbuf.at[xi], qbuf.at[xi], q_ss.at[d], q_rs.at[d], dx)
        cp.start()
        q_send.append(cp)

    def c_copy(d, src):
        p = lax.rem(me + d, PAGES)
        return remote(cbuf.at[src], cbuf.at[src], c_ss.at[d], c_rs.at[d], place(p))

    def c_start(d, c):
        c_copy(d, me).start()
        return c

    lax.fori_loop(1, PAGES, c_start, 0)
    kbuf[zi] = keys[...]
    vbuf[zi] = values[...]

    row_i = lax.broadcasted_iota(jnp.int32, (CH, CH), 0)
    col_i = lax.broadcasted_iota(jnp.int32, (CH, CH), 1)
    lower = row_i >= col_i
    tri = lower.astype(F32).astype(BF16)
    head_of = lax.broadcasted_iota(jnp.int32, (HL, FEAT), 1) // HEAD_DIM
    exp_m[...] = (head_of == lax.broadcasted_iota(jnp.int32, (HL, FEAT), 0)).astype(F32).astype(BF16)
    rate = jnp.exp(dlog[...])
    base = jnp.zeros((1, HL), F32)
    for c in range(NCH):
        sl = slice(c * CH, (c + 1) * CH)
        step = dt[sl, :]
        hi, mid, lo = split3(-step * rate)
        log = dot(tri, hi) + dot(tri, mid) + dot(tri, lo)
        middle = log[CH // 2 - 1:CH // 2, :]
        last = log[CH - 1:CH, :]
        a_hi[sl, :], a_lo[sl, :] = split2(jnp.exp(log - middle))
        b_hi[sl, :], b_lo[sl, :] = split2(jnp.exp(middle - log) * step)
        small[c:c + 1, :] = jnp.exp(last)
        small[4 + c:5 + c, :] = jnp.exp(last - middle)
        small[8 + c:9 + c, :] = jnp.exp(middle)
        small[12 + c:13 + c, :] = jnp.exp(base + middle)
        base = base + last
        bt[c] = jnp.transpose(bm[sl, :].astype(F32)).astype(BF16)
    small[16:17, :] = jnp.exp(base)
    small[17:18, :] = skip[...]
    small[18:24, :] = jnp.zeros((6, HL), F32)
    hi, mid, lo = split3(small[...])
    rows[...] = dot(hi, exp_m[...]) + dot(mid, exp_m[...]) + dot(lo, exp_m[...])

    def states(nt, carry):
        ds = pl.ds(pl.multiple_of(nt * TILE, TILE), TILE)
        e = exp_m[:, ds]
        state = None
        for c in range(NCH):
            sl = slice(c * CH, (c + 1) * CH)
            w = dot(b_hi[sl, :], e) + dot(b_lo[sl, :], e)
            xs = (x[sl, ds].astype(F32) * w).astype(BF16)
            xp[sl, ds] = xs
            fresh = rows[4 + c:5 + c, ds] * dot(bt[c], xs)
            if c == 0:
                state = fresh
            else:
                chunk_s[c - 1, :, ds] = state.astype(BF16)
                state = rows[c:c + 1, ds] * state + fresh
        sent = state.astype(BF16)
        hi, mid, lo = split3(rows[16:17, ds])
        which = lax.broadcasted_iota(jnp.int32, (16, TILE), 0)
        tail = jnp.where(
            which == 0, hi.astype(F32), jnp.where(which == 1, mid.astype(F32), jnp.where(which == 2, lo.astype(F32), 0.0))
        ).astype(BF16)
        for half in range(2):
            hs = slice(half * 128, (half + 1) * 128)
            s_send[2 * nt + half, 0:STATE, :] = sent[:, hs]
            s_send[2 * nt + half, STATE:STATE + 16, :] = tail[:, hs]
        return carry

    lax.fori_loop(0, NT, states, 0)

    def s_copy(d, src, dst):
        p = lax.rem(me + d, PAGES)
        return remote(s_send.at[src], s_recv.at[dst], s_ss.at[d], s_rs.at[d], place(p))

    def s_start(d, c):
        s_copy(d, lax.rem(me + d, PAGES), me).start()
        return c

    lax.fori_loop(1, PAGES, s_start, 0)
    s_recv[me] = s_send[me]

    for d in (1, 3, 2):
        zsrc = zpeer(4 - d)
        for i, (src, dst) in enumerate(((keys, kbuf), (values, vbuf))):
            remote(src, dst.at[zsrc], kv_ss.at[i, d], kv_rs.at[i, d], place(spot(xi, zsrc))).wait_recv()
        xsrc = xpeer(4 - d)
        remote(qbuf.at[xsrc], qbuf.at[xsrc], q_ss.at[d], q_rs.at[d], place(spot(xsrc, zi))).wait_recv()

    token_of = lax.rem(lax.broadcasted_iota(jnp.int32, (1, NQ), 1), RS)
    row_of = token_of // STEPS

    def attend(i, carry):
        queries = qbuf[i]
        first = spot(i, zi) * ROWS
        seen = jnp.zeros((1, NQ), jnp.int32)
        for r in range(ROWS):
            seen = jnp.where(row_of == r, counts[first + r], seen)
        tops = []
        for z in range(4):
            bias = jnp.where(spot(xi, z) < seen, 0.0, NEG)
            for b in range(TOK // CH):
                s = dot_t(kbuf[z, b * CH:(b + 1) * CH, :], queries) + bias
                at = z * TOK + b * CH
                scores[at:at + CH, :] = s
                tops.append(jnp.max(s.reshape(CH // 8, 8, NQ), axis=0))
        while len(tops) > 1:
            tops = [jnp.maximum(p, q) for p, q in zip(tops[::2], tops[1::2])]
        top = jnp.max(tops[0], axis=0, keepdims=True)
        total = jnp.zeros((8, NQ), F32)
        summed = jnp.zeros((ATT_DIM, NQ), F32)
        for z in range(4):
            for b in range(TOK // CH):
                at = z * TOK + b * CH
                w = jnp.exp((scores[at:at + CH, :] - top) * SCALE)
                total = total + jnp.sum(w.reshape(CH // 8, 8, NQ), axis=0)
                summed = summed + dot_tn(vbuf[z, b * CH:(b + 1) * CH, :], w.astype(BF16))
        o_send[i] = summed.astype(BF16)
        which = lax.broadcasted_iota(jnp.int32, (8, NQ), 0)
        t_send[i] = jnp.where(which == 0, top, jnp.sum(total, axis=0, keepdims=True))
        return carry

    lax.fori_loop(0, 4, attend, 0)

    o_sent = []
    for d in (1, 3, 2):
        xp_d = xpeer(d)
        dx = place(spot(xp_d, zi))
        for src, dst, ss, rs in ((o_send, o_recv, o_ss, o_rs), (t_send, t_recv, t_ss, t_rs)):
            cp = remote(src.at[xp_d], dst.at[xi], ss.at[d], rs.at[d], dx)
            cp.start()
            o_sent.append(cp)
    o_recv[xi] = o_send[xi]
    t_recv[xi] = t_send[xi]

    for c in range(NCH):
        sl = slice(c * CH, (c + 1) * CH)
        mixg[c] = jnp.where(lower, dot_t(cm[sl, :], bm[sl, :]), 0.0).astype(BF16)

    def within(nt, carry):
        ds = pl.ds(pl.multiple_of(nt * TILE, TILE), TILE)
        e = exp_m[:, ds]
        for c in range(NCH):
            sl = slice(c * CH, (c + 1) * CH)
            y = dot(mixg[c], xp[sl, ds])
            if c > 0:
                y = y + rows[8 + c:9 + c, ds] * dot(cm[sl, :], chunk_s[c - 1, :, ds])
            a = dot(a_hi[sl, :], e) + dot(a_lo[sl, :], e)
            g = gate[sl, ds].astype(F32)
            g = g / (1.0 + jnp.exp(-g))
            yi[sl, ds] = g * (a * y + rows[17:18, ds] * x[sl, ds].astype(F32))
            av[sl, ds] = g * (a * rows[12 + c:13 + c, ds])
        return carry

    lax.fori_loop(0, NT, within, 0)

    for r in range(ROWS):
        sl = slice(r * STEPS, (r + 1) * STEPS)
        flat_k[sl, :] = kd[r].astype(F32)
        flat_v[sl, :] = vd[r].astype(F32)
        flat_x[sl, :] = xd[r].astype(F32)
        flat_g[sl, :] = gd[r].astype(F32)
        flat_b[sl, :] = bd[r].astype(F32)
        flat_dt[sl, :] = dtd[r]
    key_i = lax.broadcasted_iota(jnp.int32, (RS, NQ), 0)
    tok_i = lax.rem(lax.broadcasted_iota(jnp.int32, (RS, NQ), 1), RS)
    near_ok = jnp.logical_and(key_i // STEPS == tok_i // STEPS, key_i <= tok_i)
    near = jnp.where(near_ok, dot_t(flat_k[...].astype(BF16), qbuf[xi]), NEG)
    for d in (1, 3, 2):
        xsrc = xpeer(4 - d)
        dx = place(spot(xsrc, zi))
        remote(o_send.at[xsrc], o_recv.at[xsrc], o_ss.at[d], o_rs.at[d], dx).wait_recv()
        remote(t_send.at[xsrc], t_recv.at[xsrc], t_ss.at[d], t_rs.at[d], dx).wait_recv()
    top = jnp.max(near, axis=0, keepdims=True)
    for i in range(4):
        top = jnp.maximum(top, t_recv[i, 0:1, :])
    w = jnp.where(near_ok, jnp.exp((near - top) * SCALE), 0.0)
    total = jnp.sum(w, axis=0, keepdims=True)
    summed = dot_tn(flat_v[...].astype(BF16), w.astype(BF16))
    for i in range(4):
        part = jnp.exp((t_recv[i, 0:1, :] - top) * SCALE)
        total = total + part * t_recv[i, 1:2, :]
        summed = summed + part * o_recv[i].astype(F32)
    att = jnp.transpose(summed / total)
    for h in range(QH):
        feat[me, :, FEAT + h * ATT_DIM:FEAT + (h + 1) * ATT_DIM] = att[h * RS:(h + 1) * RS, :].astype(BF16)

    def gather(start, width, s1, r1, s2, r2):
        half = width // 2
        cols = (pl.ds(start, half), pl.ds(start + half, half))

        def peer(a, d):
            return spot(xi, zpeer(d)) if a == 0 else spot(xpeer(d), zi)

        def block(p, a):
            return feat.at[p, :, cols[a]]

        sent = []

        def go(p, a, send, recv, to):
            cp = remote(block(p, a), block(p, a), send, recv, place(to))
            cp.start()
            sent.append(cp)

        def forward(p, a, k):
            for d in (1, 3, 2):
                go(p, a, s2.at[a, k, d], r2.at[a, k, d], peer(1 - a, d))

        def first():
            for d in (1, 3, 2):
                for a in (0, 1):
                    go(me, a, s1.at[a, d], r1.at[a, d], peer(a, d))
            for a in (0, 1):
                forward(me, a, 0)

        def second():
            for d in (1, 3, 2):
                for a in (0, 1):
                    p = peer(a, 4 - d)
                    remote(block(p, a), block(p, a), s1.at[a, d], r1.at[a, d], place(p)).wait_recv()
                    forward(p, a, d)

        def finish():
            for k in (0, 1, 3, 2):
                for d in (1, 3, 2):
                    for a in (0, 1):
                        if a == 0:
                            p = spot(xpeer(4 - d), zpeer(4 - k))
                            q = spot(xpeer(4 - d), zi)
                        else:
                            p = spot(xpeer(4 - k), zpeer(4 - d))
                            q = spot(xi, zpeer(4 - d))
                        remote(block(p, a), block(p, a), s2.at[a, k, d], r2.at[a, k, d], place(q)).wait_recv()

        def drain():
            for cp in sent:
                cp.wait_send()

        return first, second, finish, drain

    h_first, h_second, h_finish, h_drain = gather(FEAT, ALLF - FEAT, h1_ss, h1_rs, h2_ss, h2_rs)
    f_first, f_second, f_finish, f_drain = gather(0, FEAT, f1_ss, f1_rs, f2_ss, f2_rs)
    h_first()

    def s_wait(d, c):
        src = lax.rem(me + PAGES - d, PAGES)
        s_copy(d, src, src).wait_recv()
        return c

    lax.fori_loop(1, PAGES, s_wait, 0)
    pst[0] = jnp.zeros((STATE, 128), BF16)

    def scan(k, state):
        tail = s_recv[k, STATE:STATE + 16, :].astype(F32)
        decay = tail[0:1, :] + tail[1:2, :] + tail[2:3, :]
        state = decay * state + s_recv[k, 0:STATE, :].astype(F32)
        pst[k + 1] = state.astype(BF16)
        return state

    lax.fori_loop(0, PAGES, scan, jnp.zeros((STATE, 128), F32))

    def c_wait(d, c):
        c_copy(d, lax.rem(me + PAGES - d, PAGES)).wait_recv()
        return c

    lax.fori_loop(1, PAGES, c_wait, 0)
    h_second()

    def fill(i, c):
        which = lax.broadcasted_iota(jnp.int32, (8, 128), 0)
        cntb[pl.ds(pl.multiple_of(i * 8, 8), 8), :] = jnp.where(which < 4, counts[2 * i], counts[2 * i + 1])
        return c

    lax.fori_loop(0, PAGES * ROWS // 2, fill, 0)

    for q in range(4):
        sl = slice(q * 128, (q + 1) * 128)
        reads = cbuf[q * 4:(q + 1) * 4].reshape(128, STATE)
        want = cntb[sl, :]

        def pick(k, got):
            return jnp.where(want == k, dot(reads, pst[k]), got)

        got = lax.fori_loop(1, PAGES + 1, pick, jnp.zeros((128, 128), F32))
        sc_send[q * 4:(q + 1) * 4] = got.astype(BF16).reshape(4, RS, 128)

    def sc_copy(d, src, dst):
        p = lax.rem(me + d, PAGES)
        return remote(sc_send.at[src], sc_recv.at[dst], sc_ss.at[d], sc_rs.at[d], place(p))

    def sc_start(d, c):
        sc_copy(d, lax.rem(me + d, PAGES), me).start()
        return c

    lax.fori_loop(1, PAGES, sc_start, 0)
    sc_recv[me] = sc_send[me]

    def e_copy(d, src, dst):
        p = lax.rem(me + d, PAGES)
        return remote(pst.at[src], e_recv.at[dst], e_ss.at[d], e_rs.at[d], place(p))

    def e_start(d, c):
        e_copy(d, lax.rem(me + d, PAGES), me).start()
        return c

    lax.fori_loop(1, PAGES, e_start, 0)
    e_recv[me] = pst[me]

    tok_r = lax.broadcasted_iota(jnp.int32, (RS, RS), 0)
    tok_c = lax.broadcasted_iota(jnp.int32, (RS, RS), 1)
    same = jnp.logical_and(tok_r // STEPS == tok_c // STEPS, tok_r >= tok_c)
    same_b = same.astype(F32).astype(BF16)
    hi, mid, lo = split3(-flat_dt[...] * rate)
    log = dot(same_b, hi) + dot(same_b, mid) + dot(same_b, lo)
    ad_hi, ad_lo = split2(jnp.exp(log))
    bd_hi, bd_lo = split2(jnp.exp(-log) * flat_dt[...])
    own = jnp.where(same, dot_t(flat_c[...].astype(BF16), flat_b[...].astype(BF16)), 0.0).astype(BF16)

    def sc_wait(d, c):
        src = lax.rem(me + PAGES - d, PAGES)
        sc_copy(d, src, src).wait_recv()
        return c

    lax.fori_loop(1, PAGES, sc_wait, 0)
    square = jnp.zeros((RS, TILE), F32)
    for nt in range(NT):
        ds = slice(nt * TILE, (nt + 1) * TILE)
        e = exp_m[:, ds]
        xt = flat_x[:, ds]
        ws = (xt * (dot(bd_hi, e) + dot(bd_lo, e))).astype(BF16)
        past = jnp.concatenate([sc_recv[2 * nt], sc_recv[2 * nt + 1]], axis=1).astype(F32)
        y = (dot(ad_hi, e) + dot(ad_lo, e)) * (dot(own, ws) + past) + rows[17:18, ds] * xt
        g = flat_g[:, ds]
        u = y * (g / (1.0 + jnp.exp(-g)))
        ud[:, ds] = u
        square = square + u * u
    scale = lax.rsqrt(jnp.sum(square, axis=1, keepdims=True) * (1.0 / FEAT) + EPS)
    feat[me, :, 0:FEAT] = (ud[...] * scale * gains[...]).astype(BF16)
    f_first()

    h_finish()

    def project_att(q, c):
        lhs = feat[pl.ds(q * 4, 4), :, FEAT:ALLF].reshape(128, ALLF - FEAT)
        acc[pl.ds(pl.multiple_of(q * 128, 128), 128), :] = dot(lhs, w2[...])
        return c

    lax.fori_loop(0, 4, project_att, 0)
    f_second()

    def e_wait(d, c):
        src = lax.rem(me + PAGES - d, PAGES)
        e_copy(d, src, src).wait_recv()
        return c

    lax.fori_loop(1, PAGES, e_wait, 0)
    sq[...] = jnp.zeros((TOK, 128), F32)

    def across(nt, carry):
        ds = pl.ds(pl.multiple_of(nt * TILE, TILE), TILE)
        entry = jnp.concatenate([e_recv[2 * nt], e_recv[2 * nt + 1]], axis=1)
        for c in range(NCH):
            sl = slice(c * CH, (c + 1) * CH)
            u = yi[sl, ds] + av[sl, ds] * dot(cm[sl, :], entry)
            yi[sl, ds] = u
            u2 = u * u
            sq[sl, :] = sq[sl, :] + u2[:, 0:128] + u2[:, 128:256]
        return carry

    lax.fori_loop(0, NT, across, 0)
    fac[...] = jnp.broadcast_to(
        lax.rsqrt(jnp.sum(sq[...], axis=1, keepdims=True) * (1.0 / FEAT) + EPS), (TOK, 128)
    )

    def normed(nt, carry):
        ds = pl.ds(pl.multiple_of(nt * 128, 128), 128)
        out[:, ds] = (yi[:, ds] * fac[...] * gains[:, ds]).astype(BF16)
        return carry

    lax.fori_loop(0, FEAT // 128, normed, 0)

    f_finish()
    for q in range(4):
        sl = slice(q * 128, (q + 1) * 128)
        lhs = feat[q * 4:(q + 1) * 4, :, 0:FEAT].reshape(128, FEAT)
        part = acc[sl, :] + dot(lhs, w1[...])
        acc[sl, :] = part
        p_send[2 * q:2 * q + 2] = part.astype(BF16).reshape(2, 64, COLS)

    def p_copy(d, src, dst):
        t = lax.rem(tp + d, TP)
        return remote(p_send.at[src], p_recv.at[dst], p_ss.at[d], p_rs.at[d], {"tp": t})

    def p_start(d, c):
        p_copy(d, lax.rem(tp + d, TP), tp).start()
        return c

    lax.fori_loop(1, TP, p_start, 0)
    mine = acc[pl.ds(pl.multiple_of(tp * 64, 64), 64), :]

    def p_sum(d, got):
        src = lax.rem(tp + TP - d, TP)
        p_copy(d, src, src).wait_recv()
        return got + p_recv[src].astype(F32)

    mine = lax.fori_loop(1, TP, p_sum, mine)
    for r in range(16):
        dec[r] = mine[r * STEPS:(r + 1) * STEPS, :].astype(BF16)

    for cp in kv_send + q_send + o_sent:
        cp.wait_send()
    h_drain()
    f_drain()

    def drain(d, c):
        p = lax.rem(me + d, PAGES)
        c_copy(d, me).wait_send()
        s_copy(d, p, me).wait_send()
        sc_copy(d, p, me).wait_send()
        e_copy(d, p, me).wait_send()
        return c

    lax.fori_loop(1, PAGES, drain, 0)

    def drain_tp(d, c):
        p_copy(d, lax.rem(tp + d, TP), tp).wait_send()
        return c

    lax.fori_loop(1, TP, drain_tp, 0)


def on_device(
    prompt_mixer, prompt_gates, prompt_write, prompt_read, prompt_steps, decay_logs, skip_weights, norm_gains,
    prompt_keys, prompt_values, page_counts, decode_mixer, decode_gates, decode_write, decode_read, decode_steps,
    decode_queries, decode_keys, decode_values, mixer_output, attend_output,
):
    vmem = pl.BlockSpec(memory_space=pltpu.VMEM)
    smem = pl.BlockSpec(memory_space=pltpu.SMEM)
    v = pltpu.VMEM
    dma = pltpu.SemaphoreType.DMA
    scratch = [
        v((4, TOK, ATT_DIM), BF16), v((4, TOK, ATT_DIM), BF16), v((4, NQ, ATT_DIM), BF16),
        v((PAGES, RS, STATE), BF16),
        v((PAGES, STATE + 16, 128), BF16), v((PAGES, STATE + 16, 128), BF16),
        v((PAGES + 1, STATE, 128), BF16), v((PAGES, STATE, 128), BF16),
        v((PAGES, RS, 128), BF16), v((PAGES, RS, 128), BF16),
        v((4, ATT_DIM, NQ), BF16), v((4, ATT_DIM, NQ), BF16), v((4, 8, NQ), F32), v((4, 8, NQ), F32),
        v((PAGES, RS, ALLF), BF16), v((TP, 64, COLS), BF16), v((TP, 64, COLS), BF16),
        v((HL, FEAT), BF16), v((NCH, STATE, CH), BF16), v((NCH, CH, CH), BF16),
        v((TOK, HL), BF16), v((TOK, HL), BF16), v((TOK, HL), BF16), v((TOK, HL), BF16),
        v((24, HL), F32), v((24, FEAT), F32), v((TOK, FEAT), BF16), v((NCH - 1, STATE, FEAT), BF16),
        v((TOK, FEAT), F32), v((TOK, FEAT), F32), v((TOK, 128), F32), v((TOK, 128), F32),
        v((4 * TOK, NQ), F32), v((PAGES * RS, COLS), F32), v((PAGES * RS, 128), jnp.int32),
        v((RS, FEAT), F32), v((RS, FEAT), F32), v((RS, STATE), F32), v((RS, STATE), F32), v((RS, HL), F32),
        v((RS, QH * ATT_DIM), F32), v((RS, ATT_DIM), F32), v((RS, ATT_DIM), F32), v((RS, FEAT), F32),
        dma((2, 4)), dma((2, 4)), dma((4,)), dma((4,)), dma((PAGES,)), dma((PAGES,)),
        dma((PAGES,)), dma((PAGES,)), dma((PAGES,)), dma((PAGES,)), dma((PAGES,)), dma((PAGES,)),
        dma((4,)), dma((4,)), dma((4,)), dma((4,)),
        dma((2, 4)), dma((2, 4)), dma((2, 4, 4)), dma((2, 4, 4)),
        dma((2, 4)), dma((2, 4)), dma((2, 4, 4)), dma((2, 4, 4)),
        dma((TP,)), dma((TP,)),
    ]
    specs = [vmem] * 10 + [smem] + [vmem] * 10
    return pl.pallas_call(
        kernel,
        out_shape=(
            jax.ShapeDtypeStruct((TOK, FEAT), BF16),
            jax.ShapeDtypeStruct((16, STEPS, COLS), BF16),
        ),
        in_specs=specs,
        out_specs=(vmem, vmem),
        scratch_shapes=scratch,
        compiler_params=pltpu.CompilerParams(
            collective_id=0, has_side_effects=True, vmem_limit_bytes=60 * 2**20
        ),
        name="layers",
    )(
        prompt_mixer, prompt_gates, prompt_write, prompt_read, prompt_steps,
        decay_logs.reshape(1, HL), skip_weights.reshape(1, HL), norm_gains.reshape(1, FEAT),
        prompt_keys, prompt_values, page_counts,
        decode_mixer, decode_gates, decode_write, decode_read, decode_steps,
        decode_queries, decode_keys, decode_values, mixer_output, attend_output,
    )


def solution(mesh):
    rows, heads = ("ctx", "section"), "tp"
    split = P(rows, heads)
    split3d = P(rows, None, heads)
    return jax.shard_map(
        on_device,
        mesh=mesh,
        in_specs=(split,) * 5 + (P(heads),) * 3 + (split,) * 2 + (P(),) + (split3d,) * 8 + (P(heads, rows),) * 2,
        out_specs=(split, P(heads, None, rows)),
        check_vma=False,
    )
```

time: 1310 us -> 115 us (0.09)
  waiting for transfers between devices: 806 us -> 0 us
  matrix products: 201 us -> 0 us
  local copies, waits for them, and re-layouts: 148 us -> 5.5 us
  Pallas kernels: 0 us -> 106 us
  other arithmetic: 78.8 us -> 0 us
  blocking collectives: 48.7 us -> 0 us
  between operations: 14.7 us -> 0.65 us
    all_gather x5 -> x0, waiting for transfers between devices: 781 us -> none  [the longest x1 341 us: on_device(): lax.all_gather(after.astype(jnp.bfloat16)[None], ('ctx', 'section'), axis...]
    dot_general x19 -> x0, matrix products: 201 us -> none  [the longest x4 85.6 us: on_device(): jnp.einsum('rhn,rhpn->rhp', read_dec[:, step_index], carried, precision=H...]
    pallas_call x0 -> x1, Pallas kernels: none -> 106 us  [on_device(): pl.pallas_call(kernel, out_shape=(jax.ShapeDtypeStruct((TOK, FEAT), BF16)...]
    dynamic_update_slice x4 -> x0, local copies, waits for them, and re-layouts: 92.5 us -> none  [on_device(): lax.scan(partial(ssd_block, decay_rate, per_group), zero_state, inputs)]
    select_n x16 -> x0, other arithmetic: 56.5 us -> none  [step(): return jax.tree.map(lambda a, b: jnp.where(reached, a, b), new, before)]
    all_gather x1 -> x0, blocking collectives: 48.7 us -> none  [prefix(): lax.all_gather(part.astype(kind), axis)]
    reduce_scatter x1 -> x0, waiting for transfers between devices: 23.7 us -> none  [on_device(): lax.psum_scatter(jnp.dot(flat_rows, weight, preferred_element_type=jnp.fl...]
    reshape x7 -> x0, local copies, waits for them, and re-layouts: 17.6 us -> none  [the longest x1 6.58 us: on_device(): outputs = outputs.reshape(tokens_here, heads_here, HEAD_DIM)]
  transfers between devices with their start and end apart: 6 -> 0, of which waited for: 6 -> 0; matrix products, arithmetic and copies ran while one was open for 9% -> 0% of each run, Pallas kernels for 0% -> 0%
where the time goes in v1:
time: 115 us; the launch traced here: 113 us
  Pallas kernels  106 us (92%)
  local copies, waits for them, and re-layouts  5.5 us (5%)
    pallas_call x1, Pallas kernels, on_device(): pl.pallas_call(kernel, out_shape=(jax.ShapeDtypeStruct((TOK, FEAT), BF16)...  106 us
    unnamed x5, local copies, waits for them, and re-layouts  5.5 us

profile of v1, /device:TPU:0, one launch (start us, length us, event | category | flops | bytes accessed | tf_op | source)
XLA Modules:
  0.0 112.5 jit_solution(8909114945176750522)
XLA Ops:
  0.6 1.7 %copy.23.dt = f32[512,32]{1,0:T(8,128)} copy(f32[512,32]{0,1:T(8,128)} %param.25) | data formatting | bytes 131072 | tf_op args[4]
  2.3 106.4 %layers.1 = (bf16[512,2048]{1,0:T(8,128)(2,1)}, bf16[16,4,512]{2,1,0:T(4,128)(2,1)}) custom-call(bf16[512,2048]{1,0:T(8,128)(2,1)} %x.1, bf16[512,2048]{1,0:T(8,128)(2,1)} %gate.1, bf16[512,256]{1,0:T(8,128)(2,1)} %bm.1, bf16[512,256]{1,0:T(8,128)(2,1)} %cm.1, f32[512,32]{1,0:T(8,128)} %copy.23.dt, f32[1,32]{1,0:T(1,128)} %bitcast.4, f32[1,32]{1,0:T(1,128)} %bitcast.5, ...), custom_call_target="tpu_custom_call" | custom-call | tf_op jit(solution)/shard_map/layers/pallas_call | solution.py:590
  108.7 0.0 copy-start
  108.7 3.2 %copy.26 = bf16[512,2048]{1,0:T(8,128)(2,1)} copy(bf16[512,2048]{1,0:T(8,128)(2,1)} %get-tuple-element.4) | data formatting | bytes 4194304
  111.9 0.0 copy-done
  111.9 0.6 copy.27
Async XLA Ops:
  108.7 3.2 %copy-start = (bf16[16,4,512]{2,1,0:T(4,128)(2,1)S(1)}, bf16[16,4,512]{2,1,0:T(4,128)(2,1)}, u32[]{:S(2)}) copy-start(bf16[16,4,512]{2,1,0:T(4,128)(2,1)} %get-tuple-element.5) | copy-start | bytes 196612

commit v2 on v1

v2 whole, which is shorter than its diff:
```python
import jax
import jax.numpy as jnp
from jax import lax
from jax.experimental import pallas as pl
from jax.experimental.pallas import tpu as pltpu
from jax.sharding import PartitionSpec as P

HEADS, HEAD_DIM, STATE, GROUPS = 256, 64, 256, 8
QHEADS, KV_HEADS, ATT_DIM, STEPS = 64, 8, 128, 4
EPS = 1e-05
OFFSETS = ((2, 2), (1, 0), (0, 1), (3, 0), (0, 3), (2, 1), (1, 2), (2, 3), (3, 2), (1, 1), (3, 3), (1, 3), (3, 1), (2, 0), (0, 2))
MID = 15
NEG = -1e30
F32, BF16 = jnp.float32, jnp.bfloat16
MESH = pl.DeviceIdType.MESH

PAGES = 16
TOK = 512
HL = 32
FEAT = HL * HEAD_DIM
ROWS = 8
RS = ROWS * STEPS
CH = 128
NCH = TOK // CH
QH = QHEADS // KV_HEADS
NQ = QH * RS
TILE = 256
NT = FEAT // TILE
COLS = 512
TP = 8
ALLF = FEAT + QH * ATT_DIM
SCALE = ATT_DIM ** -0.5


def dot(a, b):
    return jnp.dot(a, b, preferred_element_type=F32)


def dot_t(a, b):
    return lax.dot_general(a, b, (((1,), (1,)), ((), ())), preferred_element_type=F32)


def dot_tn(a, b):
    return lax.dot_general(a, b, (((0,), (0,)), ((), ())), preferred_element_type=F32)


def split2(v):
    hi = v.astype(BF16)
    return hi, (v - hi.astype(F32)).astype(BF16)


def stack2(v):
    hi = v.astype(BF16).astype(F32)
    return jnp.concatenate([hi, v - hi], axis=1).astype(BF16)


def split3(v):
    hi = v.astype(BF16)
    rest = v - hi.astype(F32)
    mid = rest.astype(BF16)
    return hi, mid, (rest - mid.astype(F32)).astype(BF16)


def place(p):
    return {"ctx": p // 2, "section": lax.rem(p, 2)}


def spot(x, z):
    return (z // 2) * 8 + x * 2 + lax.rem(z, 2)


def remote(src, dst, send, recv, device):
    return pltpu.make_async_remote_copy(
        src_ref=src, dst_ref=dst, send_sem=send, recv_sem=recv, device_id=device, device_id_type=MESH
    )


def kernel(
    x_hbm, gate_hbm, bm, cm, dt_t, dlog, skip, gains, keys, values, counts,
    xd, gd, bd, cd, dtd, qd, kd, vd, w1_hbm, w2_hbm,
    out_hbm, dec,
    x, gate, w1, w2, out, in_sem, out_sem,
    kbuf, vbuf, qbuf, cbuf, s_send, s_recv, pst, e_recv, sc_send, sc_recv,
    o_send, o_recv, t_send, t_recv, feat, p_send, p_recv,
    exp_m, bt, mixg, a_w, b_w, end_w, small, rows, yi, av, sq, fac,
    scores, acc, cntb, picked, flat_x, flat_g, flat_b, flat_c, flat_dt, flat_q, flat_k, flat_v, ud,
    kv_ss, kv_rs, q_ss, q_rs, c_ss, c_rs, s_ss, s_rs, e_ss, e_rs, sc_ss, sc_rs,
    o_ss, o_rs, t_ss, t_rs, f1_ss, f1_rs, f2_ss, f2_rs, h1_ss, h1_rs, h2_ss, h2_rs, p_ss, p_rs,
):
    me = lax.axis_index("ctx") * 2 + lax.axis_index("section")
    tp = lax.axis_index("tp")
    xi = lax.rem(me // 2, 4)
    zi = (me // 8) * 2 + lax.rem(me, 2)

    def xpeer(d):
        return lax.rem(xi + d, 4)

    def zpeer(d):
        return lax.rem(zi + d, 4)

    barrier = pltpu.get_barrier_semaphore()

    class Peer:
        def __init__(self, n, dx, dz):
            self.n = n
            self.to = spot(xpeer(dx), zpeer(dz))
            self.to_place = place(self.to)
            self.back = spot(xpeer(4 - dx), zpeer(4 - dz))

    peers = [Peer(n, dx, dz) for n, (dx, dz) in enumerate(OFFSETS)]
    for peer in peers:
        pl.semaphore_signal(barrier, inc=1, device_id=peer.to_place, device_id_type=MESH)
    tpeers = [lax.rem(tp + d, TP) for d in range(1, TP)]
    for t in tpeers:
        pl.semaphore_signal(barrier, inc=1, device_id={"tp": t}, device_id_type=MESH)

    loads = [
        pltpu.make_async_copy(src, dst, in_sem.at[i])
        for i, (src, dst) in enumerate(((x_hbm, x), (gate_hbm, gate), (w2_hbm, w2), (w1_hbm, w1)))
    ]
    for cp in loads:
        cp.start()

    for r in range(ROWS):
        sl = slice(r * STEPS, (r + 1) * STEPS)
        flat_q[sl, :] = qd[r].astype(F32)
        flat_c[sl, :] = cd[r].astype(F32)
    for h in range(QH):
        qbuf[xi, h * RS:(h + 1) * RS, :] = flat_q[:, h * ATT_DIM:(h + 1) * ATT_DIM].astype(BF16)
    cbuf[me] = flat_c[...].astype(BF16)

    row_i = lax.broadcasted_iota(jnp.int32, (CH, CH), 0)
    col_i = lax.broadcasted_iota(jnp.int32, (CH, CH), 1)
    lower = row_i >= col_i
    tri = lower.astype(F32).astype(BF16)
    head_of = lax.broadcasted_iota(jnp.int32, (2 * HL, FEAT), 1) // HEAD_DIM
    head_is = lax.rem(lax.broadcasted_iota(jnp.int32, (2 * HL, FEAT), 0), HL)
    exp_m[...] = (head_of == head_is).astype(F32).astype(BF16)
    rate = jnp.exp(dlog[...])
    base = jnp.zeros((1, HL), F32)
    logs, steps = [], []
    for c in range(NCH):
        sl = slice(c * CH, (c + 1) * CH)
        step = jnp.transpose(dt_t[:, sl])
        hi, mid, lo = split3(-step * rate)
        log = dot(tri, hi) + dot(tri, mid) + dot(tri, lo)
        middle = log[CH // 2 - 1:CH // 2, :]
        last = log[CH - 1:CH, :]
        logs.append(base + log)
        steps.append(step)
        a_w[sl, :] = stack2(jnp.exp(log - middle))
        b_w[sl, :] = stack2(jnp.exp(middle - log) * step)
        small[c:c + 1, :] = jnp.exp(last)
        small[4 + c:5 + c, :] = jnp.exp(last - middle)
        small[8 + c:9 + c, :] = jnp.exp(middle)
        small[12 + c:13 + c, :] = jnp.exp(base + middle)
        base = base + last
    for c in range(NCH):
        sl = slice(c * CH, (c + 1) * CH)
        end_w[sl, :] = stack2(jnp.exp(base - logs[c]) * steps[c])
        bt[:, sl] = jnp.transpose(bm[sl, :].astype(F32)).astype(BF16)
    small[16:17, :] = jnp.exp(base)
    small[17:18, :] = skip[...]
    small[18:24, :] = jnp.zeros((6, HL), F32)
    hi, mid, lo = split3(small[...])
    one = exp_m[0:HL, :]
    rows[...] = dot(hi, one) + dot(mid, one) + dot(lo, one)

    pl.semaphore_wait(barrier, PAGES - 1 + TP - 1)

    up, down = spot(xi, zpeer(1)), spot(xi, zpeer(3))
    kv_send, q_send = [], []

    def kv(buf, n, block, to, i):
        return remote(block, buf.at[n], kv_ss.at[i], kv_rs.at[i], place(to))

    for i, (src, buf) in enumerate(((keys, kbuf), (values, vbuf))):
        for k, to in ((0, up), (1, down)):
            cp = kv(buf, zi, src, to, 2 * i + k)
            cp.start()
            kv_send.append(cp)
    for d in (1, 3, 2):
        cp = remote(qbuf.at[xi], qbuf.at[xi], q_ss.at[d], q_rs.at[d], place(spot(xpeer(d), zi)))
        cp.start()
        q_send.append(cp)
    kbuf[zi] = keys[...]
    vbuf[zi] = values[...]

    loads[0].wait()

    def states(nt, carry):
        ds = pl.ds(pl.multiple_of(nt * TILE, TILE), TILE)
        e = exp_m[:, ds]
        xs = (x[:, ds].astype(F32) * dot(end_w[...], e)).astype(BF16)
        state = dot(bt[...], xs)
        sent = state.astype(BF16)
        hi, mid, lo = split3(rows[16:17, ds])
        which = lax.broadcasted_iota(jnp.int32, (16, TILE), 0)
        tail = jnp.where(
            which == 0, hi.astype(F32), jnp.where(which == 1, mid.astype(F32), jnp.where(which == 2, lo.astype(F32), 0.0))
        ).astype(BF16)
        for half in range(2):
            hs = slice(half * 128, (half + 1) * 128)
            s_send[2 * nt + half, 0:STATE, :] = sent[:, hs]
            s_send[2 * nt + half, STATE:STATE + 16, :] = tail[:, hs]
        return carry

    lax.fori_loop(0, NT, states, 0)

    kv(kbuf, zpeer(3), keys, up, 0).wait_recv()
    cp = kv(kbuf, zpeer(3), kbuf.at[zpeer(3)], up, 4)
    cp.start()
    kv_send.append(cp)
    kv(vbuf, zpeer(1), values, down, 3).wait_recv()
    cp = kv(vbuf, zpeer(1), vbuf.at[zpeer(1)], down, 5)
    cp.start()
    kv_send.append(cp)

    def exchange(src, dst, send, recv):
        def copy(peer):
            return remote(src.at[peer.to], dst.at[me], send.at[peer.n], recv.at[peer.n], peer.to_place)

        def landed(peer):
            remote(src.at[peer.back], dst.at[peer.back], send.at[peer.n], recv.at[peer.n], place(peer.back)).wait_recv()

        return copy, landed

    s_copy, s_landed = exchange(s_send, s_recv, s_ss, s_rs)
    sc_copy, sc_landed = exchange(sc_send, sc_recv, sc_ss, sc_rs)
    e_copy, e_landed = exchange(pst, e_recv, e_ss, e_rs)

    def c_copy(peer, src):
        return remote(cbuf.at[src], cbuf.at[src], c_ss.at[peer.n], c_rs.at[peer.n], peer.to_place)

    for peer in peers:
        s_copy(peer).start()
    for peer in peers:
        c_copy(peer, me).start()
    s_recv[me] = s_send[me]

    kv(kbuf, zpeer(1), keys, down, 1).wait_recv()
    kv(vbuf, zpeer(3), values, up, 2).wait_recv()
    kv(kbuf, zpeer(2), keys, up, 4).wait_recv()
    kv(vbuf, zpeer(2), values, down, 5).wait_recv()
    for d in (1, 3, 2):
        xsrc = xpeer(4 - d)
        remote(qbuf.at[xsrc], qbuf.at[xsrc], q_ss.at[d], q_rs.at[d], place(spot(xsrc, zi))).wait_recv()

    token_of = lax.rem(lax.broadcasted_iota(jnp.int32, (1, NQ), 1), RS)
    row_of = token_of // STEPS

    def attend(i, carry):
        queries = qbuf[i]
        first = spot(i, zi) * ROWS
        seen = jnp.zeros((1, NQ), jnp.int32)
        for r in range(ROWS):
            seen = jnp.where(row_of == r, counts[first + r], seen)
        tops = []
        for z in range(4):
            bias = jnp.where(spot(xi, z) < seen, 0.0, NEG)
            for b in range(TOK // CH):
                s = dot_t(kbuf[z, b * CH:(b + 1) * CH, :], queries) + bias
                at = z * TOK + b * CH
                scores[at:at + CH, :] = s
                tops.append(jnp.max(s.reshape(CH // 8, 8, NQ), axis=0))
        while len(tops) > 1:
            tops = [jnp.maximum(p, q) for p, q in zip(tops[::2], tops[1::2])]
        top = jnp.max(tops[0], axis=0, keepdims=True)
        total = jnp.zeros((8, NQ), F32)
        summed = jnp.zeros((ATT_DIM, NQ), F32)
        for z in range(4):
            for b in range(TOK // CH):
                at = z * TOK + b * CH
                w = jnp.exp((scores[at:at + CH, :] - top) * SCALE)
                total = total + jnp.sum(w.reshape(CH // 8, 8, NQ), axis=0)
                summed = summed + dot_tn(vbuf[z, b * CH:(b + 1) * CH, :], w.astype(BF16))
        o_send[i] = summed.astype(BF16)
        which = lax.broadcasted_iota(jnp.int32, (8, NQ), 0)
        t_send[i] = jnp.where(which == 0, top, jnp.sum(total, axis=0, keepdims=True))
        return carry

    lax.fori_loop(0, 4, attend, 0)

    o_sent = []
    for d in (1, 3, 2):
        xp_d = xpeer(d)
        dx = place(spot(xp_d, zi))
        for src, dst, ss, rs in ((o_send, o_recv, o_ss, o_rs), (t_send, t_recv, t_ss, t_rs)):
            cp = remote(src.at[xp_d], dst.at[xi], ss.at[d], rs.at[d], dx)
            cp.start()
            o_sent.append(cp)
    o_recv[xi] = o_send[xi]
    t_recv[xi] = t_send[xi]

    for peer in peers:
        c_copy(peer, peer.back).wait_recv()

    def fill(i, c):
        which = lax.broadcasted_iota(jnp.int32, (8, 128), 0)
        cntb[pl.ds(pl.multiple_of(i * 8, 8), 8), :] = jnp.where(which < 4, counts[2 * i], counts[2 * i + 1])
        return c

    lax.fori_loop(0, PAGES * ROWS // 2, fill, 0)

    def mask_reads(k, c):
        for q in range(4):
            sl = slice(q * 128, (q + 1) * 128)
            reads = cbuf[q * 4:(q + 1) * 4].reshape(128, STATE).astype(F32)
            want = cntb[sl, :] == k + 1
            for half in range(2):
                hs = slice(half * 128, (half + 1) * 128)
                at = pl.ds(pl.multiple_of(k * STATE + half * 128, 128), 128)
                picked[sl, at] = jnp.where(want, reads[:, hs], 0.0).astype(BF16)
        return c

    lax.fori_loop(0, PAGES, mask_reads, 0)

    for r in range(ROWS):
        sl = slice(r * STEPS, (r + 1) * STEPS)
        flat_k[sl, :] = kd[r].astype(F32)
        flat_v[sl, :] = vd[r].astype(F32)
        flat_x[sl, :] = xd[r].astype(F32)
        flat_g[sl, :] = gd[r].astype(F32)
        flat_b[sl, :] = bd[r].astype(F32)
        flat_dt[sl, :] = dtd[r]
    key_i = lax.broadcasted_iota(jnp.int32, (RS, NQ), 0)
    tok_i = lax.rem(lax.broadcasted_iota(jnp.int32, (RS, NQ), 1), RS)
    near_ok = jnp.logical_and(key_i // STEPS == tok_i // STEPS, key_i <= tok_i)
    near = jnp.where(near_ok, dot_t(flat_k[...].astype(BF16), qbuf[xi]), NEG)
    for d in (1, 3, 2):
        xsrc = xpeer(4 - d)
        dx = place(spot(xsrc, zi))
        remote(o_send.at[xsrc], o_recv.at[xsrc], o_ss.at[d], o_rs.at[d], dx).wait_recv()
        remote(t_send.at[xsrc], t_recv.at[xsrc], t_ss.at[d], t_rs.at[d], dx).wait_recv()
    top = jnp.max(near, axis=0, keepdims=True)
    for i in range(4):
        top = jnp.maximum(top, t_recv[i, 0:1, :])
    w = jnp.where(near_ok, jnp.exp((near - top) * SCALE), 0.0)
    total = jnp.sum(w, axis=0, keepdims=True)
    summed = dot_tn(flat_v[...].astype(BF16), w.astype(BF16))
    for i in range(4):
        part = jnp.exp((t_recv[i, 0:1, :] - top) * SCALE)
        total = total + part * t_recv[i, 1:2, :]
        summed = summed + part * o_recv[i].astype(F32)
    att = jnp.transpose(summed / total)
    for h in range(QH):
        feat[me, :, FEAT + h * ATT_DIM:FEAT + (h + 1) * ATT_DIM] = att[h * RS:(h + 1) * RS, :].astype(BF16)

    def gather(start, width, s1, r1, s2, r2):
        half = width // 2
        cols = (pl.ds(start, half), pl.ds(start + half, half))

        def peer(a, d):
            return spot(xi, zpeer(d)) if a == 0 else spot(xpeer(d), zi)

        def block(p, a):
            return feat.at[p, :, cols[a]]

        sent = []

        def go(p, a, send, recv, to):
            cp = remote(block(p, a), block(p, a), send, recv, place(to))
            cp.start()
            sent.append(cp)

        def forward(p, a, k):
            for d in (1, 3, 2):
                go(p, a, s2.at[a, k, d], r2.at[a, k, d], peer(1 - a, d))

        def first():
            for d in (1, 3, 2):
                for a in (0, 1):
                    go(me, a, s1.at[a, d], r1.at[a, d], peer(a, d))
            for a in (0, 1):
                forward(me, a, 0)

        def second():
            for d in (1, 3, 2):
                for a in (0, 1):
                    p = peer(a, 4 - d)
                    remote(block(p, a), block(p, a), s1.at[a, d], r1.at[a, d], place(p)).wait_recv()
                    forward(p, a, d)

        def finish():
            for k in (0, 1, 3, 2):
                for d in (1, 3, 2):
                    for a in (0, 1):
                        if a == 0:
                            p = spot(xpeer(4 - d), zpeer(4 - k))
                            q = spot(xpeer(4 - d), zi)
                        else:
                            p = spot(xpeer(4 - k), zpeer(4 - d))
                            q = spot(xi, zpeer(4 - d))
                        remote(block(p, a), block(p, a), s2.at[a, k, d], r2.at[a, k, d], place(q)).wait_recv()

        def drain():
            for cp in sent:
                cp.wait_send()

        return first, second, finish, drain

    h_first, h_second, h_finish, h_drain = gather(FEAT, ALLF - FEAT, h1_ss, h1_rs, h2_ss, h2_rs)
    f_first, f_second, f_finish, f_drain = gather(0, FEAT, f1_ss, f1_rs, f2_ss, f2_rs)
    h_first()

    tok_r = lax.broadcasted_iota(jnp.int32, (RS, RS), 0)
    tok_c = lax.broadcasted_iota(jnp.int32, (RS, RS), 1)
    same = jnp.logical_and(tok_r // STEPS == tok_c // STEPS, tok_r >= tok_c)
    same_b = same.astype(F32).astype(BF16)
    hi, mid, lo = split3(-flat_dt[...] * rate)
    log = dot(same_b, hi) + dot(same_b, mid) + dot(same_b, lo)
    ad_w = stack2(jnp.exp(log))
    bd_w = stack2(jnp.exp(-log) * flat_dt[...])
    own = jnp.where(same, dot_t(flat_c[...].astype(BF16), flat_b[...].astype(BF16)), 0.0).astype(BF16)

    for nt in range(NT):
        ds = slice(nt * TILE, (nt + 1) * TILE)
        e = exp_m[:, ds]
        xt = flat_x[:, ds]
        ws = (xt * dot(bd_w, e)).astype(BF16)
        g = flat_g[:, ds]
        g = g / (1.0 + jnp.exp(-g))
        a = dot(ad_w, e)
        ud[:, ds] = g * (a * dot(own, ws) + rows[17:18, ds] * xt)
        flat_g[:, ds] = g * a

    for peer in peers:
        s_landed(peer)
    pst[0] = jnp.zeros((STATE, 128), BF16)

    def scan(k, state):
        tail = s_recv[k, STATE:STATE + 16, :].astype(F32)
        decay = tail[0:1, :] + tail[1:2, :] + tail[2:3, :]
        state = decay * state + s_recv[k, 0:STATE, :].astype(F32)
        pst[k + 1] = state.astype(BF16)
        return state

    lax.fori_loop(0, PAGES, scan, jnp.zeros((STATE, 128), F32), unroll=4)

    for q in range(2):
        sl = slice(q * 256, (q + 1) * 256)
        got = dot(picked[sl, :], pst[1:PAGES + 1].reshape(PAGES * STATE, 128))
        sc_send[q * 8:(q + 1) * 8] = got.astype(BF16).reshape(8, RS, 128)

    for peer in peers:
        sc_copy(peer).start()
    sc_recv[me] = sc_send[me]

    h_second()
    e_recv[me] = pst[me]

    for peer in peers:
        sc_landed(peer)
    square = jnp.zeros((RS, TILE), F32)
    for nt in range(NT):
        ds = slice(nt * TILE, (nt + 1) * TILE)
        past = jnp.concatenate([sc_recv[2 * nt], sc_recv[2 * nt + 1]], axis=1).astype(F32)
        u = ud[:, ds] + flat_g[:, ds] * past
        ud[:, ds] = u
        square = square + u * u
    scale = lax.rsqrt(jnp.sum(square, axis=1, keepdims=True) * (1.0 / FEAT) + EPS)
    feat[me, :, 0:FEAT] = (ud[...] * scale * gains[...]).astype(BF16)
    f_first()

    loads[1].wait()
    for c in range(NCH):
        sl = slice(c * CH, (c + 1) * CH)
        mixg[c] = jnp.where(lower, dot_t(cm[sl, :], bm[sl, :]), 0.0).astype(BF16)

    def within(nt, carry):
        ds = pl.ds(pl.multiple_of(nt * TILE, TILE), TILE)
        e = exp_m[:, ds]
        state = None
        for c in range(NCH):
            sl = slice(c * CH, (c + 1) * CH)
            xf = x[sl, ds].astype(F32)
            xs = (xf * dot(b_w[sl, :], e)).astype(BF16)
            y = dot(mixg[c], xs)
            if c > 0:
                y = y + rows[8 + c:9 + c, ds] * dot(cm[sl, :], state.astype(BF16))
            if c < NCH - 1:
                fresh = rows[4 + c:5 + c, ds] * dot(bt[:, sl], xs)
                state = fresh if c == 0 else rows[c:c + 1, ds] * state + fresh
            a = dot(a_w[sl, :], e)
            g = gate[sl, ds].astype(F32)
            g = g / (1.0 + jnp.exp(-g))
            yi[sl, ds] = g * (a * y + rows[17:18, ds] * xf)
            av[sl, ds] = g * (a * rows[12 + c:13 + c, ds])
        return carry

    lax.fori_loop(0, NT // 2, within, 0)
    f_second()
    for peer in peers[:MID]:
        e_copy(peer).start()
    lax.fori_loop(NT // 2, NT, within, 0)

    h_finish()
    loads[2].wait()

    def project_att(q, c):
        lhs = feat[pl.ds(q * 4, 4), :, FEAT:ALLF].reshape(128, ALLF - FEAT)
        acc[pl.ds(pl.multiple_of(q * 128, 128), 128), :] = dot(lhs, w2[...])
        return c

    lax.fori_loop(0, 4, project_att, 0)
    loads[3].wait()

    f_finish()

    def p_copy(d, src, dst):
        t = lax.rem(tp + d, TP)
        return remote(p_send.at[src], p_recv.at[dst], p_ss.at[d], p_rs.at[d], {"tp": t})

    for turn in (1, 3, 2, 0):
        q = lax.rem(tp // 2 + turn, 4)
        at = pl.ds(pl.multiple_of(q * 128, 128), 128)
        lhs = feat[pl.ds(q * 4, 4), :, 0:FEAT].reshape(128, FEAT)
        part = acc[at, :] + dot(lhs, w1[...])
        if turn == 0:
            acc[at, :] = part
        p_send[pl.ds(2 * q, 2)] = part.astype(BF16).reshape(2, 64, COLS)
        for half in range(2):
            t = 2 * q + half
            d = lax.rem(t - tp + TP, TP)
            if turn == 0:
                @pl.when(d != 0)
                def _():
                    p_copy(d, t, tp).start()
            else:
                p_copy(d, t, tp).start()

    for peer in peers[MID:]:
        e_copy(peer).start()
    sq[...] = jnp.zeros((TOK, 128), F32)
    for n in range(PAGES):
        if n > 0:
            e_landed(peers[n - 1])
        src = me if n == 0 else peers[n - 1].back
        ds = pl.ds(pl.multiple_of(src * 128, 128), 128)
        entry = e_recv[src]
        for c in range(NCH):
            sl = slice(c * CH, (c + 1) * CH)
            u = yi[sl, ds] + av[sl, ds] * dot(cm[sl, :], entry)
            yi[sl, ds] = u
            sq[sl, :] = sq[sl, :] + u * u
    fac[...] = jnp.broadcast_to(
        lax.rsqrt(jnp.sum(sq[...], axis=1, keepdims=True) * (1.0 / FEAT) + EPS), (TOK, 128)
    )

    writes = []
    for c in range(NCH):
        sl = slice(c * CH, (c + 1) * CH)

        def normed(nt, carry, sl=sl):
            ds = pl.ds(pl.multiple_of(nt * 128, 128), 128)
            out[sl, ds] = (yi[sl, ds] * fac[sl, :] * gains[:, ds]).astype(BF16)
            return carry

        lax.fori_loop(0, FEAT // 128, normed, 0)
        cp = pltpu.make_async_copy(out.at[sl], out_hbm.at[sl], out_sem.at[c])
        cp.start()
        writes.append(cp)

    mine = acc[pl.ds(pl.multiple_of(tp * 64, 64), 64), :]

    def p_sum(d, got):
        src = lax.rem(tp + TP - d, TP)
        p_copy(d, src, src).wait_recv()
        return got + p_recv[src].astype(F32)

    mine = lax.fori_loop(1, TP, p_sum, mine)
    for r in range(16):
        dec[r] = mine[r * STEPS:(r + 1) * STEPS, :].astype(BF16)

    for cp in writes:
        cp.wait()
    for cp in kv_send + q_send + o_sent:
        cp.wait_send()
    h_drain()
    f_drain()

    for peer in peers:
        for cp in (s_copy(peer), c_copy(peer, me), sc_copy(peer), e_copy(peer)):
            cp.wait_send()

    def drain_tp(d, c):
        p_copy(d, lax.rem(tp + d, TP), tp).wait_send()
        return c

    lax.fori_loop(1, TP, drain_tp, 0)


def on_device(
    prompt_mixer, prompt_gates, prompt_write, prompt_read, prompt_steps, decay_logs, skip_weights, norm_gains,
    prompt_keys, prompt_values, page_counts, decode_mixer, decode_gates, decode_write, decode_read, decode_steps,
    decode_queries, decode_keys, decode_values, mixer_output, attend_output,
):
    vmem = pl.BlockSpec(memory_space=pltpu.VMEM)
    smem = pl.BlockSpec(memory_space=pltpu.SMEM)
    v = pltpu.VMEM
    dma = pltpu.SemaphoreType.DMA
    scratch = [
        v((TOK, FEAT), BF16), v((TOK, FEAT), BF16), v((FEAT, COLS), BF16), v((ALLF - FEAT, COLS), BF16),
        v((TOK, FEAT), BF16), dma((4,)), dma((4,)),
        v((4, TOK, ATT_DIM), BF16), v((4, TOK, ATT_DIM), BF16), v((4, NQ, ATT_DIM), BF16),
        v((PAGES, RS, STATE), BF16),
        v((PAGES, STATE + 16, 128), BF16), v((PAGES, STATE + 16, 128), BF16),
        v((PAGES + 1, STATE, 128), BF16), v((PAGES, STATE, 128), BF16),
        v((PAGES, RS, 128), BF16), v((PAGES, RS, 128), BF16),
        v((4, ATT_DIM, NQ), BF16), v((4, ATT_DIM, NQ), BF16), v((4, 8, NQ), F32), v((4, 8, NQ), F32),
        v((PAGES, RS, ALLF), BF16), v((TP, 64, COLS), BF16), v((TP, 64, COLS), BF16),
        v((2 * HL, FEAT), BF16), v((STATE, TOK), BF16), v((NCH, CH, CH), BF16),
        v((TOK, 2 * HL), BF16), v((TOK, 2 * HL), BF16), v((TOK, 2 * HL), BF16),
        v((24, HL), F32), v((24, FEAT), F32),
        v((TOK, FEAT), F32), v((TOK, FEAT), F32), v((TOK, 128), F32), v((TOK, 128), F32),
        v((4 * TOK, NQ), F32), v((PAGES * RS, COLS), F32), v((PAGES * RS, 128), jnp.int32),
        v((PAGES * RS, PAGES * STATE), BF16),
        v((RS, FEAT), F32), v((RS, FEAT), F32), v((RS, STATE), F32), v((RS, STATE), F32), v((RS, HL), F32),
        v((RS, QH * ATT_DIM), F32), v((RS, ATT_DIM), F32), v((RS, ATT_DIM), F32), v((RS, FEAT), F32),
        dma((6,)), dma((6,)), dma((4,)), dma((4,)), dma((PAGES,)), dma((PAGES,)),
        dma((PAGES,)), dma((PAGES,)), dma((PAGES,)), dma((PAGES,)), dma((PAGES,)), dma((PAGES,)),
        dma((4,)), dma((4,)), dma((4,)), dma((4,)),
        dma((2, 4)), dma((2, 4)), dma((2, 4, 4)), dma((2, 4, 4)),
        dma((2, 4)), dma((2, 4)), dma((2, 4, 4)), dma((2, 4, 4)),
        dma((TP,)), dma((TP,)),
    ]
    hbm = pl.BlockSpec(memory_space=pl.ANY)
    specs = [hbm] * 2 + [vmem] * 8 + [smem] + [vmem] * 8 + [hbm] * 2
    return pl.pallas_call(
        kernel,
        out_shape=(
            jax.ShapeDtypeStruct((TOK, FEAT), BF16),
            jax.ShapeDtypeStruct((16, STEPS, COLS), BF16),
        ),
        in_specs=specs,
        out_specs=(hbm, vmem),
        scratch_shapes=scratch,
        compiler_params=pltpu.CompilerParams(
            collective_id=0, has_side_effects=True, vmem_limit_bytes=60 * 2**20
        ),
        name="layers",
    )(
        prompt_mixer, prompt_gates, prompt_write, prompt_read, prompt_steps.T,
        decay_logs.reshape(1, HL), skip_weights.reshape(1, HL), norm_gains.reshape(1, FEAT),
        prompt_keys, prompt_values, page_counts,
        decode_mixer, decode_gates, decode_write, decode_read, decode_steps,
        decode_queries, decode_keys, decode_values, mixer_output, attend_output,
    )


def solution(mesh):
    rows, heads = ("ctx", "section"), "tp"
    split = P(rows, heads)
    split3d = P(rows, None, heads)
    return jax.shard_map(
        on_device,
        mesh=mesh,
        in_specs=(split,) * 5 + (P(heads),) * 3 + (split,) * 2 + (P(),) + (split3d,) * 8 + (P(heads, rows),) * 2,
        out_specs=(split, P(heads, None, rows)),
        check_vma=False,
    )
```

time: 115 us -> 90.3 us (0.79); the launches traced: 113 us -> 90.1 us
  Pallas kernels: 106 us -> 85.7 us
  local copies, waits for them, and re-layouts: 5.5 us -> 3.82 us
    pallas_call x1, Pallas kernels: 106 us -> 85.7 us  [on_device(): pl.pallas_call(kernel, out_shape=(jax.ShapeDtypeStruct((TOK, FEAT), BF16)...]
    unnamed x5 -> x4, local copies, waits for them, and re-layouts: 5.5 us -> 3.82 us
where the time goes in v2:
time: 90.3 us; the launch traced here: 90.1 us
  Pallas kernels  85.7 us (95%)
  local copies, waits for them, and re-layouts  3.82 us (4%)
    pallas_call x1, Pallas kernels, on_device(): pl.pallas_call(kernel, out_shape=(jax.ShapeDtypeStruct((TOK, FEAT), BF16)...  85.7 us
    unnamed x4, local copies, waits for them, and re-layouts  3.82 us

profile of v2, /device:TPU:0, one launch (start us, length us, event | category | flops | bytes accessed | tf_op | source)
XLA Modules:
  0.0 90.1 jit_solution(1341254466713579274)
XLA Ops:
  0.6 85.7 %layers.1 = (bf16[512,2048]{1,0:T(8,128)(2,1)}, bf16[16,4,512]{2,1,0:T(4,128)(2,1)}) custom-call(bf16[512,2048]{1,0:T(8,128)(2,1)} %x_hbm.1, bf16[512,2048]{1,0:T(8,128)(2,1)} %gate_hbm.1, bf16[512,256]{1,0:T(8,128)(2,1)} %bm.1, bf16[512,256]{1,0:T(8,128)(2,1)} %cm.1, f32[32,512]{1,0:T(8,128)} %bitcast.4, f32[1,32]{1,0:T(1,128)} %bitcast.6, ...), custom_call_target="tpu_custom_call" | custom-call | tf_op jit(solution)/shard_map/layers/pallas_call | solution.py:629
  86.3 0.0 copy-start
  86.3 3.2 %copy.25 = bf16[512,2048]{1,0:T(8,128)(2,1)} copy(bf16[512,2048]{1,0:T(8,128)(2,1)} %get-tuple-element.4) | data formatting | bytes 4194304
  89.5 0.0 copy-done
  89.5 0.6 copy.26
Async XLA Ops:
  86.3 3.2 %copy-start = (bf16[16,4,512]{2,1,0:T(4,128)(2,1)S(1)}, bf16[16,4,512]{2,1,0:T(4,128)(2,1)}, u32[]{:S(2)}) copy-start(bf16[16,4,512]{2,1,0:T(4,128)(2,1)} %get-tuple-element.5) | copy-start | bytes 196612

commit v3 on v2

v3 whole, which is shorter than its diff:
```python
import jax
import jax.numpy as jnp
from jax import lax
from jax.experimental import pallas as pl
from jax.experimental.pallas import tpu as pltpu
from jax.sharding import PartitionSpec as P

HEADS, HEAD_DIM, STATE, GROUPS = 256, 64, 256, 8
QHEADS, KV_HEADS, ATT_DIM, STEPS = 64, 8, 128, 4
EPS = 1e-05
OFFSETS = ((2, 2), (1, 0), (0, 1), (3, 0), (0, 3), (2, 1), (1, 2), (2, 3), (3, 2), (1, 1), (3, 3), (1, 3), (3, 1), (2, 0), (0, 2))
NEG = -1e30
F32, BF16 = jnp.float32, jnp.bfloat16
MESH = pl.DeviceIdType.MESH

PAGES = 16
TOK = 512
HL = 32
FEAT = HL * HEAD_DIM
ROWS = 8
RS = ROWS * STEPS
CH = 128
NCH = TOK // CH
QH = QHEADS // KV_HEADS
NQ = QH * RS
TILE = 256
NT = FEAT // TILE
COLS = 512
TP = 8
ALLF = FEAT + QH * ATT_DIM
SCALE = ATT_DIM ** -0.5


def dot(a, b):
    return jnp.dot(a, b, preferred_element_type=F32)


def dot_t(a, b):
    return lax.dot_general(a, b, (((1,), (1,)), ((), ())), preferred_element_type=F32)


def dot_tn(a, b):
    return lax.dot_general(a, b, (((0,), (0,)), ((), ())), preferred_element_type=F32)


def split2(v):
    hi = v.astype(BF16)
    return hi, (v - hi.astype(F32)).astype(BF16)


def stack2(v):
    hi = v.astype(BF16).astype(F32)
    return jnp.concatenate([hi, v - hi], axis=1).astype(BF16)


def split3(v):
    hi = v.astype(BF16)
    rest = v - hi.astype(F32)
    mid = rest.astype(BF16)
    return hi, mid, (rest - mid.astype(F32)).astype(BF16)


def spot(x, z):
    return lax.div(z, 2) * 8 + x * 2 + lax.rem(z, 2)


def remote(src, dst, send, recv, device):
    return pltpu.make_async_remote_copy(
        src_ref=src, dst_ref=dst, send_sem=send, recv_sem=recv, device_id=device, device_id_type=MESH
    )


def kernel(
    x_hbm, gate_hbm, bm_hbm, cm_hbm, dt_hbm, dlog_hbm, skip_hbm, gains_hbm, keys_hbm, values_hbm, counts,
    xd_hbm, gd_hbm, bd_hbm, cd_hbm, dtd_hbm, qd_hbm, kd_hbm, vd_hbm, w1_hbm, w2_hbm,
    out_hbm, dec,
    bm, cm, dt_t, dlog, skip, gains, keys, values, xd, gd, bd, cd, dtd, qd, kd, vd, small_sem,
    x, gate, w1, w2, out, in_sem, out_sem,
    kbuf, vbuf, qbuf, cbuf, s_send, s_recv, pst, e_recv, sc_send, sc_recv,
    o_send, o_recv, t_send, t_recv, feat, p_send, p_recv, r_send, r_recv,
    exp_m, bt, mixg, a_w, b_w, end_w, small, rows, yi, av, sq, fac,
    scores, acc, cntb, picked, flat_x, flat_g, flat_b, flat_c, flat_dt, flat_q, flat_k, flat_v, ud,
    kv_ss, kv_rs, q_ss, q_rs, c_ss, c_rs, s_ss, s_rs, e_ss, e_rs, sc_ss, sc_rs,
    o_ss, o_rs, t_ss, t_rs, f1_ss, f1_rs, f2_ss, f2_rs, h1_ss, h1_rs, h2_ss, h2_rs, p_ss, p_rs, r_ss, r_rs,
):
    ctx, section = lax.axis_index("ctx"), lax.axis_index("section")
    tp = lax.axis_index("tp")
    me = ctx * 2 + section
    xi = lax.rem(ctx, 4)
    zi = lax.div(ctx, 4) * 2 + section
    xs = [xi] + [lax.rem(xi + d, 4) for d in range(1, 4)]
    zs = [zi] + [lax.rem(zi + d, 4) for d in range(1, 4)]
    z_ctx = [lax.div(z, 2) * 4 for z in zs]
    z_section = [lax.rem(z, 2) for z in zs]
    known = {}

    def off(dx, dz):
        key = (dx % 4, dz % 4)
        if key not in known:
            c = z_ctx[key[1]] + xs[key[0]]
            known[key] = (c * 2 + z_section[key[1]], {"ctx": c, "section": z_section[key[1]]})
        return known[key]

    def xpeer(d):
        return xs[d % 4]

    def zpeer(d):
        return zs[d % 4]

    ready = [
        pltpu.make_async_copy(src, dst, small_sem.at[i])
        for i, (src, dst) in enumerate((
            (qd_hbm, qd), (cd_hbm, cd), (keys_hbm, keys), (values_hbm, values), (dt_hbm, dt_t), (dlog_hbm, dlog),
            (skip_hbm, skip), (gains_hbm, gains), (bm_hbm, bm), (cm_hbm, cm), (xd_hbm, xd), (gd_hbm, gd), (bd_hbm, bd),
            (dtd_hbm, dtd), (kd_hbm, kd), (vd_hbm, vd),
        ))
    ]
    for cp in ready:
        cp.start()

    barrier = pltpu.get_barrier_semaphore()

    class Peer:
        def __init__(self, n, dx, dz):
            self.n = n
            self.to, self.to_place = off(dx, dz)
            self.back, self.back_place = off(-dx, -dz)

    peers = [Peer(n, dx, dz) for n, (dx, dz) in enumerate(OFFSETS)]
    for peer in peers:
        pl.semaphore_signal(barrier, inc=1, device_id=peer.to_place, device_id_type=MESH)
    tpeers = [lax.rem(tp + d, TP) for d in range(1, TP)]
    for t in tpeers:
        pl.semaphore_signal(barrier, inc=1, device_id={"tp": t}, device_id_type=MESH)

    loads = [
        pltpu.make_async_copy(src, dst, in_sem.at[i])
        for i, (src, dst) in enumerate(((x_hbm, x), (gate_hbm, gate), (w2_hbm, w2), (w1_hbm, w1)))
    ]
    for cp in loads:
        cp.start()

    for cp in ready:
        cp.wait()

    for r in range(ROWS):
        sl = slice(r * STEPS, (r + 1) * STEPS)
        flat_q[sl, :] = qd[r].astype(F32)
        flat_c[sl, :] = cd[r].astype(F32)
    for h in range(QH):
        qbuf[xi, h * RS:(h + 1) * RS, :] = flat_q[:, h * ATT_DIM:(h + 1) * ATT_DIM].astype(BF16)
    cbuf[me] = flat_c[...].astype(BF16)

    row_i = lax.broadcasted_iota(jnp.int32, (CH, CH), 0)
    col_i = lax.broadcasted_iota(jnp.int32, (CH, CH), 1)
    lower = row_i >= col_i
    tri = lower.astype(F32).astype(BF16)
    lane = lax.broadcasted_iota(jnp.int32, (2 * HL, FEAT), 1)
    head = lax.broadcasted_iota(jnp.int32, (2 * HL, FEAT), 0)
    start = jnp.where(head < HL, head, head - HL) * HEAD_DIM
    inside = jnp.logical_and(lane >= start, lane < start + HEAD_DIM)
    exp_m[...] = jnp.where(inside, 1.0, 0.0).astype(BF16)
    rate = jnp.exp(dlog[...])
    base = jnp.zeros((1, HL), F32)
    logs, steps = [], []
    for c in range(NCH):
        sl = slice(c * CH, (c + 1) * CH)
        step = jnp.transpose(dt_t[:, sl])
        hi, mid, lo = split3(-step * rate)
        log = dot(tri, hi) + dot(tri, mid) + dot(tri, lo)
        middle = log[CH // 2 - 1:CH // 2, :]
        last = log[CH - 1:CH, :]
        logs.append(base + log)
        steps.append(step)
        a_w[sl, :] = stack2(jnp.exp(log - middle))
        b_w[sl, :] = stack2(jnp.exp(middle - log) * step)
        small[c:c + 1, :] = jnp.exp(last)
        small[4 + c:5 + c, :] = jnp.exp(last - middle)
        small[8 + c:9 + c, :] = jnp.exp(middle)
        small[12 + c:13 + c, :] = jnp.exp(base + middle)
        base = base + last
    for c in range(NCH):
        sl = slice(c * CH, (c + 1) * CH)
        end_w[sl, :] = stack2(jnp.exp(base - logs[c]) * steps[c])
        bt[:, sl] = jnp.transpose(bm[sl, :].astype(F32)).astype(BF16)
    small[16:17, :] = jnp.exp(base)
    small[17:18, :] = skip[...]
    small[18:24, :] = jnp.zeros((6, HL), F32)
    hi, mid, lo = split3(small[...])
    one = exp_m[0:HL, :]
    rows[...] = dot(hi, one) + dot(mid, one) + dot(lo, one)

    pl.semaphore_wait(barrier, PAGES - 1 + TP - 1)

    up, down = off(0, 1)[1], off(0, 3)[1]
    kv_send, q_send = [], []

    def kv(buf, n, block, to, i):
        return remote(block, buf.at[n], kv_ss.at[i], kv_rs.at[i], to)


    loads[0].wait()

    def states(nt, carry):
        ds = pl.ds(pl.multiple_of(nt * TILE, TILE), TILE)
        e = exp_m[:, ds]
        xs = (x[:, ds].astype(F32) * dot(end_w[...], e)).astype(BF16)
        state = dot(bt[...], xs)
        sent = state.astype(BF16)
        hi, mid, lo = split3(rows[16:17, ds])
        which = lax.broadcasted_iota(jnp.int32, (16, TILE), 0)
        tail = jnp.where(
            which == 0, hi.astype(F32), jnp.where(which == 1, mid.astype(F32), jnp.where(which == 2, lo.astype(F32), 0.0))
        ).astype(BF16)
        for half in range(2):
            hs = slice(half * 128, (half + 1) * 128)
            s_send[2 * nt + half, 0:STATE, :] = sent[:, hs]
            s_send[2 * nt + half, STATE:STATE + 16, :] = tail[:, hs]
        return carry

    lax.fori_loop(0, NT, states, 0)

    def exchange(src, dst, send, recv):
        def copy(peer):
            return remote(src.at[peer.to], dst.at[me], send.at[peer.n], recv.at[peer.n], peer.to_place)

        def landed(peer):
            remote(src.at[peer.back], dst.at[peer.back], send.at[peer.n], recv.at[peer.n], peer.back_place).wait_recv()

        return copy, landed

    s_copy, s_landed = exchange(s_send, s_recv, s_ss, s_rs)
    sc_copy, sc_landed = exchange(sc_send, sc_recv, sc_ss, sc_rs)
    e_copy, e_landed = exchange(pst, e_recv, e_ss, e_rs)

    def c_copy(peer, src):
        return remote(cbuf.at[src], cbuf.at[src], c_ss.at[peer.n], c_rs.at[peer.n], peer.to_place)

    for peer in peers:
        s_copy(peer).start()
    for peer in peers:
        c_copy(peer, me).start()
    s_recv[me] = s_send[me]
    for d in (1, 3, 2):
        cp = remote(qbuf.at[xi], qbuf.at[xi], q_ss.at[d], q_rs.at[d], off(d, 0)[1])
        cp.start()
        q_send.append(cp)

    loads[1].wait()
    for c in range(NCH):
        sl = slice(c * CH, (c + 1) * CH)
        mixg[c] = jnp.where(lower, dot_t(cm[sl, :], bm[sl, :]), 0.0).astype(BF16)

    def within(nt, carry):
        ds = pl.ds(pl.multiple_of(nt * TILE, TILE), TILE)
        e = exp_m[:, ds]
        state = None
        for c in range(NCH):
            sl = slice(c * CH, (c + 1) * CH)
            xf = x[sl, ds].astype(F32)
            xs = (xf * dot(b_w[sl, :], e)).astype(BF16)
            y = dot(mixg[c], xs)
            if c > 0:
                y = y + rows[8 + c:9 + c, ds] * dot(cm[sl, :], state.astype(BF16))
            if c < NCH - 1:
                fresh = rows[4 + c:5 + c, ds] * dot(bt[:, sl], xs)
                state = fresh if c == 0 else rows[c:c + 1, ds] * state + fresh
            a = dot(a_w[sl, :], e)
            g = gate[sl, ds].astype(F32)
            g = g / (1.0 + jnp.exp(-g))
            yi[sl, ds] = g * (a * y + rows[17:18, ds] * xf)
            av[sl, ds] = g * (a * rows[12 + c:13 + c, ds])
        return carry

    lax.fori_loop(0, NT, within, 0)

    for peer in peers:
        c_copy(peer, peer.back).wait_recv()

    def fill(i, c):
        which = lax.broadcasted_iota(jnp.int32, (8, 128), 0)
        cntb[pl.ds(pl.multiple_of(i * 8, 8), 8), :] = jnp.where(which < 4, counts[2 * i], counts[2 * i + 1])
        return c

    lax.fori_loop(0, PAGES * ROWS // 2, fill, 0)

    def mask_reads(k, c):
        for q in range(4):
            sl = slice(q * 128, (q + 1) * 128)
            reads = cbuf[q * 4:(q + 1) * 4].reshape(128, STATE).astype(F32)
            want = cntb[sl, :] == k + 1
            for half in range(2):
                hs = slice(half * 128, (half + 1) * 128)
                at = pl.ds(pl.multiple_of(k * STATE + half * 128, 128), 128)
                picked[sl, at] = jnp.where(want, reads[:, hs], 0.0).astype(BF16)
        return c

    lax.fori_loop(0, PAGES, mask_reads, 0)

    for r in range(ROWS):
        sl = slice(r * STEPS, (r + 1) * STEPS)
        flat_k[sl, :] = kd[r].astype(F32)
        flat_v[sl, :] = vd[r].astype(F32)
        flat_x[sl, :] = xd[r].astype(F32)
        flat_g[sl, :] = gd[r].astype(F32)
        flat_b[sl, :] = bd[r].astype(F32)
        flat_dt[sl, :] = dtd[r]
    tok_r = lax.broadcasted_iota(jnp.int32, (RS, RS), 0)
    tok_c = lax.broadcasted_iota(jnp.int32, (RS, RS), 1)
    same = jnp.logical_and(tok_r // STEPS == tok_c // STEPS, tok_r >= tok_c)
    same_b = same.astype(F32).astype(BF16)
    hi, mid, lo = split3(-flat_dt[...] * rate)
    log = dot(same_b, hi) + dot(same_b, mid) + dot(same_b, lo)
    ad_w = stack2(jnp.exp(log))
    bd_w = stack2(jnp.exp(-log) * flat_dt[...])
    own = jnp.where(same, dot_t(flat_c[...].astype(BF16), flat_b[...].astype(BF16)), 0.0).astype(BF16)

    for nt in range(NT):
        ds = slice(nt * TILE, (nt + 1) * TILE)
        e = exp_m[:, ds]
        xt = flat_x[:, ds]
        ws = (xt * dot(bd_w, e)).astype(BF16)
        g = flat_g[:, ds]
        g = g / (1.0 + jnp.exp(-g))
        a = dot(ad_w, e)
        ud[:, ds] = g * (a * dot(own, ws) + rows[17:18, ds] * xt)
        flat_g[:, ds] = g * a

    def gather(start, width, s1, r1, s2, r2):
        half = width // 2
        cols = (pl.ds(start, half), pl.ds(start + half, half))

        def peer(a, d):
            return off(0, d) if a == 0 else off(d, 0)

        def block(p, a):
            return feat.at[p, :, cols[a]]

        sent = []

        def go(p, a, send, recv, to):
            cp = remote(block(p, a), block(p, a), send, recv, to[1])
            cp.start()
            sent.append(cp)

        def forward(p, a, k):
            for d in (1, 3, 2):
                go(p, a, s2.at[a, k, d], r2.at[a, k, d], peer(1 - a, d))

        def first():
            for d in (1, 3, 2):
                for a in (0, 1):
                    go(me, a, s1.at[a, d], r1.at[a, d], peer(a, d))
            for a in (0, 1):
                forward(me, a, 0)

        def second():
            for d in (1, 3, 2):
                for a in (0, 1):
                    p, where = peer(a, -d)
                    remote(block(p, a), block(p, a), s1.at[a, d], r1.at[a, d], where).wait_recv()
                    forward(p, a, d)

        def finish():
            for k in (0, 1, 3, 2):
                for d in (1, 3, 2):
                    for a in (0, 1):
                        p = (off(-d, -k) if a == 0 else off(-k, -d))[0]
                        where = peer(1 - a, -d)[1]
                        remote(block(p, a), block(p, a), s2.at[a, k, d], r2.at[a, k, d], where).wait_recv()

        def drain():
            for cp in sent:
                cp.wait_send()

        return first, second, finish, drain

    h_first, h_second, h_finish, h_drain = gather(FEAT, ALLF - FEAT, h1_ss, h1_rs, h2_ss, h2_rs)
    f_first, f_second, f_finish, f_drain = gather(0, FEAT, f1_ss, f1_rs, f2_ss, f2_rs)
    for peer in peers:
        s_landed(peer)
    for i, (src, buf) in enumerate(((keys, kbuf), (values, vbuf))):
        for k, to in ((0, up), (1, down)):
            cp = kv(buf, zi, src, to, 2 * i + k)
            cp.start()
            kv_send.append(cp)
    kbuf[zi] = keys[...]
    vbuf[zi] = values[...]
    pst[0] = jnp.zeros((STATE, 128), BF16)

    def scan(k, state):
        tail = s_recv[k, STATE:STATE + 16, :].astype(F32)
        decay = tail[0:1, :] + tail[1:2, :] + tail[2:3, :]
        state = decay * state + s_recv[k, 0:STATE, :].astype(F32)
        pst[k + 1] = state.astype(BF16)
        return state

    lax.fori_loop(0, PAGES, scan, jnp.zeros((STATE, 128), F32), unroll=4)

    for q in range(2):
        sl = slice(q * 256, (q + 1) * 256)
        got = dot(picked[sl, :], pst[1:PAGES + 1].reshape(PAGES * STATE, 128))
        sc_send[q * 8:(q + 1) * 8] = got.astype(BF16).reshape(8, RS, 128)

    for peer in peers:
        sc_copy(peer).start()
    sc_recv[me] = sc_send[me]

    kv(kbuf, zpeer(3), keys, up, 0).wait_recv()
    cp = kv(kbuf, zpeer(3), kbuf.at[zpeer(3)], up, 4)
    cp.start()
    kv_send.append(cp)
    kv(vbuf, zpeer(1), values, down, 3).wait_recv()
    cp = kv(vbuf, zpeer(1), vbuf.at[zpeer(1)], down, 5)
    cp.start()
    kv_send.append(cp)

    e_recv[me] = pst[me]

    for peer in peers:
        sc_landed(peer)
    square = jnp.zeros((RS, TILE), F32)
    for nt in range(NT):
        ds = slice(nt * TILE, (nt + 1) * TILE)
        past = jnp.concatenate([sc_recv[2 * nt], sc_recv[2 * nt + 1]], axis=1).astype(F32)
        u = ud[:, ds] + flat_g[:, ds] * past
        ud[:, ds] = u
        square = square + u * u
    scale = lax.rsqrt(jnp.sum(square, axis=1, keepdims=True) * (1.0 / FEAT) + EPS)
    feat[me, :, 0:FEAT] = (ud[...] * scale * gains[...]).astype(BF16)
    f_first()

    kv(kbuf, zpeer(1), keys, down, 1).wait_recv()
    kv(vbuf, zpeer(3), values, up, 2).wait_recv()
    kv(kbuf, zpeer(2), keys, up, 4).wait_recv()
    kv(vbuf, zpeer(2), values, down, 5).wait_recv()
    for d in (1, 3, 2):
        xsrc = xpeer(4 - d)
        remote(qbuf.at[xsrc], qbuf.at[xsrc], q_ss.at[d], q_rs.at[d], off(-d, 0)[1]).wait_recv()

    token_of = lax.rem(lax.broadcasted_iota(jnp.int32, (1, NQ), 1), RS)
    row_of = token_of // STEPS

    def attend(i, carry):
        queries = qbuf[i]
        first = spot(i, zi) * ROWS
        seen = jnp.zeros((1, NQ), jnp.int32)
        for r in range(ROWS):
            seen = jnp.where(row_of == r, counts[first + r], seen)
        tops = []
        for z in range(4):
            bias = jnp.where(spot(xi, z) < seen, 0.0, NEG)
            for b in range(TOK // CH):
                s = dot_t(kbuf[z, b * CH:(b + 1) * CH, :], queries) + bias
                at = z * TOK + b * CH
                scores[at:at + CH, :] = s
                tops.append(jnp.max(s.reshape(CH // 8, 8, NQ), axis=0))
        while len(tops) > 1:
            tops = [jnp.maximum(p, q) for p, q in zip(tops[::2], tops[1::2])]
        top = jnp.max(tops[0], axis=0, keepdims=True)
        total = jnp.zeros((8, NQ), F32)
        summed = jnp.zeros((ATT_DIM, NQ), F32)
        for z in range(4):
            for b in range(TOK // CH):
                at = z * TOK + b * CH
                w = jnp.exp((scores[at:at + CH, :] - top) * SCALE)
                total = total + jnp.sum(w.reshape(CH // 8, 8, NQ), axis=0)
                summed = summed + dot_tn(vbuf[z, b * CH:(b + 1) * CH, :], w.astype(BF16))
        o_send[i] = summed.astype(BF16)
        which = lax.broadcasted_iota(jnp.int32, (8, NQ), 0)
        t_send[i] = jnp.where(which == 0, top, jnp.sum(total, axis=0, keepdims=True))
        return carry

    lax.fori_loop(0, 2, attend, 0)
    f_second()
    for peer in peers:
        e_copy(peer).start()
    lax.fori_loop(2, 4, attend, 0)

    o_sent = []
    for d in (1, 3, 2):
        xp_d = xpeer(d)
        dx = off(d, 0)[1]
        for src, dst, ss, rs in ((o_send, o_recv, o_ss, o_rs), (t_send, t_recv, t_ss, t_rs)):
            cp = remote(src.at[xp_d], dst.at[xi], ss.at[d], rs.at[d], dx)
            cp.start()
            o_sent.append(cp)
    o_recv[xi] = o_send[xi]
    t_recv[xi] = t_send[xi]

    f_finish()
    loads[3].wait()

    def project(q, c):
        lhs = feat[pl.ds(q * 4, 4), :, 0:FEAT].reshape(128, FEAT)
        acc[pl.ds(pl.multiple_of(q * 128, 128), 128), :] = dot(lhs, w1[...])
        return c

    lax.fori_loop(0, 4, project, 0)

    key_i = lax.broadcasted_iota(jnp.int32, (RS, NQ), 0)
    tok_i = lax.rem(lax.broadcasted_iota(jnp.int32, (RS, NQ), 1), RS)
    near_ok = jnp.logical_and(key_i // STEPS == tok_i // STEPS, key_i <= tok_i)
    near = jnp.where(near_ok, dot_t(flat_k[...].astype(BF16), qbuf[xi]), NEG)
    for d in (1, 3, 2):
        xsrc = xpeer(4 - d)
        dx = off(-d, 0)[1]
        remote(o_send.at[xsrc], o_recv.at[xsrc], o_ss.at[d], o_rs.at[d], dx).wait_recv()
        remote(t_send.at[xsrc], t_recv.at[xsrc], t_ss.at[d], t_rs.at[d], dx).wait_recv()
    top = jnp.max(near, axis=0, keepdims=True)
    for i in range(4):
        top = jnp.maximum(top, t_recv[i, 0:1, :])
    w = jnp.where(near_ok, jnp.exp((near - top) * SCALE), 0.0)
    total = jnp.sum(w, axis=0, keepdims=True)
    summed = dot_tn(flat_v[...].astype(BF16), w.astype(BF16))
    for i in range(4):
        part = jnp.exp((t_recv[i, 0:1, :] - top) * SCALE)
        total = total + part * t_recv[i, 1:2, :]
        summed = summed + part * o_recv[i].astype(F32)
    att = jnp.transpose(summed / total)
    for h in range(QH):
        feat[me, :, FEAT + h * ATT_DIM:FEAT + (h + 1) * ATT_DIM] = att[h * RS:(h + 1) * RS, :].astype(BF16)

    h_first()

    sq[...] = jnp.zeros((TOK, 128), F32)

    def across(n):
        if n > 0:
            e_landed(peers[n - 1])
        src = me if n == 0 else peers[n - 1].back
        ds = pl.ds(pl.multiple_of(src * 128, 128), 128)
        entry = e_recv[src]
        for c in range(NCH):
            sl = slice(c * CH, (c + 1) * CH)
            u = yi[sl, ds] + av[sl, ds] * dot(cm[sl, :], entry)
            yi[sl, ds] = u
            sq[sl, :] = sq[sl, :] + u * u

    for n in range(8):
        across(n)
    h_second()
    for n in range(8, PAGES):
        across(n)

    h_finish()
    loads[2].wait()

    core, yi_here = lax.rem(tp, 2), lax.div(tp, 2)
    order = (1, 3, 2, 0)

    def p1_copy(turn, q):
        return remote(
            p_send.at[2 * q + 1 - core], p_recv.at[turn], p_ss.at[turn], p_rs.at[turn], {"tp": 2 * yi_here + 1 - core}
        )

    def p2_copy(turn, q):
        return remote(r_send.at[turn], r_recv.at[turn], r_ss.at[turn], r_rs.at[turn], {"tp": 2 * q + core})

    def both_cores(turn, q):
        p1_copy(turn, q).wait_recv()
        return acc[pl.ds(pl.multiple_of((2 * q + core) * 64, 64), 64), :] + p_recv[turn].astype(F32)

    owners = [lax.rem(yi_here + turn, 4) for turn in range(4)]
    for turn in order:
        q = owners[turn]
        at = pl.ds(pl.multiple_of(q * 128, 128), 128)
        lhs = feat[pl.ds(q * 4, 4), :, FEAT:ALLF].reshape(128, ALLF - FEAT)
        part = acc[at, :] + dot(lhs, w2[...])
        acc[at, :] = part
        p_send[pl.ds(2 * q, 2)] = part.astype(BF16).reshape(2, 64, COLS)
        p1_copy(turn, q).start()
    for turn in order[:3]:
        r_send[turn] = both_cores(turn, owners[turn]).astype(BF16)
        p2_copy(turn, owners[turn]).start()

    fac[...] = jnp.broadcast_to(
        lax.rsqrt(jnp.sum(sq[...], axis=1, keepdims=True) * (1.0 / FEAT) + EPS), (TOK, 128)
    )

    writes = []
    for c in range(NCH):
        sl = slice(c * CH, (c + 1) * CH)

        def normed(nt, carry, sl=sl):
            ds = pl.ds(pl.multiple_of(nt * 128, 128), 128)
            out[sl, ds] = (yi[sl, ds] * fac[sl, :] * gains[:, ds]).astype(BF16)
            return carry

        lax.fori_loop(0, FEAT // 128, normed, 0)
        cp = pltpu.make_async_copy(out.at[sl], out_hbm.at[sl], out_sem.at[c])
        cp.start()
        writes.append(cp)

    mine = both_cores(0, owners[0])
    for turn in order[:3]:
        p2_copy(turn, owners[turn]).wait_recv()
        mine = mine + r_recv[turn].astype(F32)
    for r in range(16):
        dec[r] = mine[r * STEPS:(r + 1) * STEPS, :].astype(BF16)

    for cp in writes:
        cp.wait()
    for cp in kv_send + q_send + o_sent:
        cp.wait_send()
    h_drain()
    f_drain()

    for peer in peers:
        for cp in (s_copy(peer), c_copy(peer, me), sc_copy(peer), e_copy(peer)):
            cp.wait_send()

    for turn in order:
        p1_copy(turn, owners[turn]).wait_send()
        if turn > 0:
            p2_copy(turn, owners[turn]).wait_send()


def hand_over(a, b, a_out, b_out, a_held, b_held, in_sem, out_sem):
    rows = TOK // 8
    slices = [pl.ds(i * rows, rows) for i in range(8)]
    pairs = [(a.at[sl], a_held.at[sl], a_out.at[sl]) for sl in slices] + [(b, b_held, b_out)]
    inward = [pltpu.make_async_copy(src, held, in_sem.at[i]) for i, (src, held, _) in enumerate(pairs)]
    outward = [pltpu.make_async_copy(held, dst, out_sem.at[i]) for i, (_, held, dst) in enumerate(pairs)]
    for cp in inward:
        cp.start()
    for arrived, leaving in zip(inward, outward):
        arrived.wait()
        leaving.start()
    for cp in outward:
        cp.wait()


def on_device(
    prompt_mixer, prompt_gates, prompt_write, prompt_read, prompt_steps, decay_logs, skip_weights, norm_gains,
    prompt_keys, prompt_values, page_counts, decode_mixer, decode_gates, decode_write, decode_read, decode_steps,
    decode_queries, decode_keys, decode_values, mixer_output, attend_output,
):
    vmem = pl.BlockSpec(memory_space=pltpu.VMEM)
    smem = pl.BlockSpec(memory_space=pltpu.SMEM)
    v = pltpu.VMEM
    dma = pltpu.SemaphoreType.DMA
    scratch = [
        v((TOK, STATE), BF16), v((TOK, STATE), BF16), v((HL, TOK), F32), v((1, HL), F32), v((1, HL), F32), v((1, FEAT), F32),
        v((TOK, ATT_DIM), BF16), v((TOK, ATT_DIM), BF16),
        v((ROWS, STEPS, FEAT), BF16), v((ROWS, STEPS, FEAT), BF16),
        v((ROWS, STEPS, STATE), BF16), v((ROWS, STEPS, STATE), BF16), v((ROWS, STEPS, HL), F32),
        v((ROWS, STEPS, QH * ATT_DIM), BF16), v((ROWS, STEPS, ATT_DIM), BF16), v((ROWS, STEPS, ATT_DIM), BF16), dma((16,)),
        v((TOK, FEAT), BF16), v((TOK, FEAT), BF16), v((FEAT, COLS), BF16), v((ALLF - FEAT, COLS), BF16),
        v((TOK, FEAT), BF16), dma((4,)), dma((4,)),
        v((4, TOK, ATT_DIM), BF16), v((4, TOK, ATT_DIM), BF16), v((4, NQ, ATT_DIM), BF16),
        v((PAGES, RS, STATE), BF16),
        v((PAGES, STATE + 16, 128), BF16), v((PAGES, STATE + 16, 128), BF16),
        v((PAGES + 1, STATE, 128), BF16), v((PAGES, STATE, 128), BF16),
        v((PAGES, RS, 128), BF16), v((PAGES, RS, 128), BF16),
        v((4, ATT_DIM, NQ), BF16), v((4, ATT_DIM, NQ), BF16), v((4, 8, NQ), F32), v((4, 8, NQ), F32),
        v((PAGES, RS, ALLF), BF16), v((TP, 64, COLS), BF16),
        v((4, 64, COLS), BF16), v((4, 64, COLS), BF16), v((4, 64, COLS), BF16),
        v((2 * HL, FEAT), BF16), v((STATE, TOK), BF16), v((NCH, CH, CH), BF16),
        v((TOK, 2 * HL), BF16), v((TOK, 2 * HL), BF16), v((TOK, 2 * HL), BF16),
        v((24, HL), F32), v((24, FEAT), F32),
        v((TOK, FEAT), F32), v((TOK, FEAT), F32), v((TOK, 128), F32), v((TOK, 128), F32),
        v((4 * TOK, NQ), F32), v((PAGES * RS, COLS), F32), v((PAGES * RS, 128), jnp.int32),
        v((PAGES * RS, PAGES * STATE), BF16),
        v((RS, FEAT), F32), v((RS, FEAT), F32), v((RS, STATE), F32), v((RS, STATE), F32), v((RS, HL), F32),
        v((RS, QH * ATT_DIM), F32), v((RS, ATT_DIM), F32), v((RS, ATT_DIM), F32), v((RS, FEAT), F32),
        dma((6,)), dma((6,)), dma((4,)), dma((4,)), dma((PAGES,)), dma((PAGES,)),
        dma((PAGES,)), dma((PAGES,)), dma((PAGES,)), dma((PAGES,)), dma((PAGES,)), dma((PAGES,)),
        dma((4,)), dma((4,)), dma((4,)), dma((4,)),
        dma((2, 4)), dma((2, 4)), dma((2, 4, 4)), dma((2, 4, 4)),
        dma((2, 4)), dma((2, 4)), dma((2, 4, 4)), dma((2, 4, 4)),
        dma((4,)), dma((4,)), dma((4,)), dma((4,)),
    ]
    hbm = pl.BlockSpec(memory_space=pl.ANY)
    specs = [hbm] * 10 + [smem] + [hbm] * 10
    shapes = (jax.ShapeDtypeStruct((TOK, FEAT), BF16), jax.ShapeDtypeStruct((16, STEPS, COLS), BF16))
    results = pl.pallas_call(
        kernel,
        out_shape=shapes,
        in_specs=specs,
        out_specs=(hbm, vmem),
        scratch_shapes=scratch,
        compiler_params=pltpu.CompilerParams(
            collective_id=0, has_side_effects=True, vmem_limit_bytes=60 * 2**20
        ),
        name="layers",
    )(
        prompt_mixer, prompt_gates, prompt_write, prompt_read, prompt_steps.T,
        decay_logs.reshape(1, HL), skip_weights.reshape(1, HL), norm_gains.reshape(1, FEAT),
        prompt_keys, prompt_values, page_counts,
        decode_mixer, decode_gates, decode_write, decode_read, decode_steps,
        decode_queries, decode_keys, decode_values, mixer_output, attend_output,
    )
    return pl.pallas_call(
        hand_over,
        out_shape=shapes,
        in_specs=[hbm, hbm],
        out_specs=(hbm, hbm),
        scratch_shapes=[v((TOK, FEAT), BF16), v((16, STEPS, COLS), BF16), dma((9,)), dma((9,))],
        name="results",
    )(*results)


def solution(mesh):
    rows, heads = ("ctx", "section"), "tp"
    split = P(rows, heads)
    split3d = P(rows, None, heads)
    return jax.shard_map(
        on_device,
        mesh=mesh,
        in_specs=(split,) * 5 + (P(heads),) * 3 + (split,) * 2 + (P(),) + (split3d,) * 8 + (P(heads, rows),) * 2,
        out_specs=(split, P(heads, None, rows)),
        check_vma=False,
    )
```

time: 90.3 us -> 98.1 us (1.086)
  Pallas kernels: 85.7 us -> 96.6 us
  local copies, waits for them, and re-layouts: 3.82 us -> 0 us
    pallas_call x1 -> x2, Pallas kernels: 85.7 us -> 96.6 us  [the longest x1 94.2 us: on_device(): pl.pallas_call(kernel, out_shape=shapes, in_specs=specs, out_specs=(hbm,...]
    unnamed x4 -> x0, local copies, waits for them, and re-layouts: 3.82 us -> none
where the time goes in v3:
time: 98.1 us; the launch traced here: 97.3 us
  Pallas kernels  96.6 us (98%)
    pallas_call x1, Pallas kernels, on_device(): pl.pallas_call(kernel, out_shape=shapes, in_specs=specs, out_specs=(hbm,...  94.2 us
    pallas_call x1, Pallas kernels, on_device(): pl.pallas_call(hand_over, out_shape=shapes, in_specs=[hbm, hbm], out_spec...  2.43 us

profile of v3, /device:TPU:0, one launch (start us, length us, event | category | flops | bytes accessed | tf_op | source)
XLA Modules:
  0.0 97.3 jit_solution(1188873419210402209)
XLA Ops:
  0.6 94.2 %layers.1 = (bf16[512,2048]{1,0:T(8,128)(2,1)}, bf16[16,4,512]{2,1,0:T(4,128)(2,1)}) custom-call(bf16[512,2048]{1,0:T(8,128)(2,1)} %x_hbm.1, bf16[512,2048]{1,0:T(8,128)(2,1)} %gate_hbm.1, bf16[512,256]{1,0:T(8,128)(2,1)} %bm_hbm.1, bf16[512,256]{1,0:T(8,128)(2,1)} %cm_hbm.1, f32[32,512]{1,0:T(8,128)} %bitcast.4, f32[1,32]{1,0:T(1,128)} %bitcast.6, ...), custom_call_target="tpu_custom_call" | custom-call | tf_op jit(solution)/shard_map/layers/pallas_call | solution.py:677
  94.8 2.4 %results.1 = (bf16[512,2048]{1,0:T(8,128)(2,1)}, bf16[16,4,512]{2,1,0:T(4,128)(2,1)}) custom-call(bf16[512,2048]{1,0:T(8,128)(2,1)} %get-tuple-element.4.a, bf16[16,4,512]{2,1,0:T(4,128)(2,1)} %get-tuple-element.5.b), custom_call_target="tpu_custom_call" | custom-call | tf_op jit(solution)/shard_map/results/pallas_call | solution.py:694
